TPU v7x, 32 devices: a whole 2x2x4 slice. The times are simulated.
32 devices in a mesh: pool: 2 (over x), context: 8 (over z, y), tensor: 2 (over core).
Axes of the slice: x: 2, y: 2, z: 4, core: 2. Of those that a mesh axis runs over, the one named last changes fastest.
Arguments:
- cache: bfloat16 [2, 8, 16, 576], P('pool', 'context'), may hold values from -6 to 6
- hit_slots: int32 [2, 8], P('pool'), may hold values from 0 to 7, each once within a row
- prefix_blocks: int32 [2], P('pool'), may hold values from 2 to 8, as said below
- suffix_len: int32 [2], P('pool'), may hold values from 128 to 512, as said below
- suffix_latent: bfloat16 [2, 512, 576], P('pool', 'context')
- suffix_query: bfloat16 [2, 512, 64, 576], P('pool', 'context', 'tensor')
- decode_hidden: bfloat16 [2, 2, 7168], P('pool'), may hold values from -6 to 6
- kv_down: bfloat16 [7168, 576], P(('context', 'tensor')), may hold values from -0.0625 to 0.0625
- kv_gain: float32 [512], replicated, may hold values from 0.1 to 1.9
- decode_query: bfloat16 [2, 2, 64, 576], P('pool', None, 'tensor')
Outputs:
- suffix_context: bfloat16 [2, 512, 64, 512], P('pool', 'context', 'tensor')
- decode_context: bfloat16 [2, 2, 64, 512], P('pool', None, 'tensor')
- decode_latent: bfloat16 [2, 2, 576], P('pool')
Inputs may be any that keep to these rules, and one draw needn't show every extreme that they name: `prefix_blocks`: some request has all of its group's 8 slots as hits. `suffix_len`: some request has all 512 suffix tokens valid.
All inputs are finite; a program needn't handle non-finite values.
Results may differ from a plain program's by a relative error of at most 0.03.
Values may be sent and summed in bfloat16 or wider, within the bound.
No kernel may reach another device: no remote copies, remote signals or barrier semaphores. Data moves between devices by JAX's collectives and lax.ppermute only.
A program may use at most 128 MiB of HBM per device.

v0:
```python
import math

import jax
import jax.numpy as jnp
from jax import lax
from jax.sharding import PartitionSpec as P

SCALE = 192.0 ** (-0.5)
NEG = -1e30


def attend(state, queries, key_rows, allowed):
    running_max, running_sum, accum = state
    lat_width = accum.shape[-1]
    scores = (
        jnp.einsum("rhc,kc->rhk", queries, key_rows, preferred_element_type=jnp.float32) * SCALE
    )
    scores = jnp.where(allowed[:, None, :], scores, NEG)
    new_max = jnp.maximum(running_max, jnp.max(scores, axis=-1))
    rescale = jnp.exp(running_max - new_max)
    weights = jnp.where(allowed[:, None, :], jnp.exp(scores - new_max[..., None]), 0.0).astype(
        jnp.bfloat16
    )
    running_sum = running_sum * rescale + jnp.sum(weights.astype(jnp.float32), axis=-1)
    accum = accum * rescale[..., None] + jnp.einsum(
        "rhk,kc->rhc", weights, key_rows[:, :lat_width], preferred_element_type=jnp.float32
    )
    return (new_max, running_sum, accum)


def attend_blocks(state, queries, key_rows, allowed):
    key_count = key_rows.shape[0]
    span_size = math.gcd(key_count, 512)
    if span_size == key_count:
        return attend(state, queries, key_rows, allowed)
    block_count = key_count // span_size
    key_blocks = key_rows.reshape(block_count, span_size, key_rows.shape[1])
    allow_blocks = jnp.moveaxis(allowed.reshape(allowed.shape[0], block_count, span_size), 1, 0)

    def advance(carry, item):
        return (attend(carry, queries, item[0], item[1]), None)

    state, unused = lax.scan(advance, state, (key_blocks, allow_blocks))
    return state


def fresh_state(row_count, heads, lat_width):
    return (
        jnp.full((row_count, heads), NEG, jnp.float32),
        jnp.zeros((row_count, heads), jnp.float32),
        jnp.zeros((row_count, heads, lat_width), jnp.float32),
    )


def rotate_latent(raw, kv_gain, positions):
    lat_width = kv_gain.shape[0]
    latent = raw[:, :lat_width]
    normed = latent * lax.rsqrt(jnp.mean(latent * latent, axis=-1, keepdims=True) + 1e-06) * kv_gain
    half = (raw.shape[1] - lat_width) // 2
    freq = 10000.0 ** (-jnp.arange(half, dtype=jnp.float32) / half)
    angle = positions[:, None] * freq[None, :]
    first = raw[:, lat_width : lat_width + half]
    second = raw[:, lat_width + half :]
    cosine = jnp.cos(angle)
    sine = jnp.sin(angle)
    rotated = jnp.concatenate(
        [first * cosine - second * sine, second * cosine + first * sine], axis=-1
    )
    return jnp.concatenate([normed, rotated], axis=-1).astype(jnp.bfloat16)


def finish(state):
    return (state[2] / state[1][..., None]).astype(jnp.bfloat16)


def on_device(
    cache,
    hit_slots,
    prefix_blocks,
    suffix_len,
    suffix_latent,
    suffix_query,
    decode_hidden,
    kv_down,
    kv_gain,
    decode_query,
):
    lat_width = kv_gain.shape[0]
    slot_total = hit_slots.shape[1]
    block_rows = cache.shape[2]
    kv_width = cache.shape[3]
    ctx_rank = lax.axis_index("context")
    slot_ids = jnp.arange(slot_total, dtype=jnp.int32)
    slot_live = jnp.any(
        (hit_slots[0][:, None] == slot_ids[None, :]) & (slot_ids < prefix_blocks[0])[:, None],
        axis=0,
    )
    queries = suffix_query[0]
    tok_count = queries.shape[0]
    heads = queries.shape[1]
    tok_ids = ctx_rank * tok_count + jnp.arange(tok_count, dtype=jnp.int32)
    last_token = ctx_rank * tok_count + tok_count - 1
    dec_queries = decode_query[0]
    dec_count = dec_queries.shape[0]
    dec_ids = jnp.arange(dec_count, dtype=jnp.int32)
    suffix_end = suffix_len[0]
    row_count = kv_down.shape[0]
    part_index = lax.axis_index(("context", "tensor"))
    hidden_part = lax.dynamic_slice_in_dim(decode_hidden[0], part_index * row_count, row_count, 1)
    raw = lax.psum(
        jnp.dot(hidden_part, kv_down, preferred_element_type=jnp.float32), ("context", "tensor")
    )
    positions = (prefix_blocks[0] * block_rows + suffix_end + dec_ids).astype(jnp.float32)
    fresh = rotate_latent(raw, kv_gain, positions)
    states = (fresh_state(tok_count, heads, lat_width), fresh_state(dec_count, heads, lat_width))
    key_rows = lax.all_gather(suffix_latent, "context", axis=1, tiled=True)[0]
    key_count = key_rows.shape[0]
    key_ids = jnp.arange(key_count, dtype=jnp.int32)

    def visit(tok_carry):
        tok_allow = key_ids[None, :] <= tok_ids[:, None]
        return attend_blocks(tok_carry, queries, key_rows, tok_allow)

    def leave(tok_carry):
        return tok_carry

    tok_state = lax.cond(jnp.int32(0) <= last_token, visit, leave, states[0])
    dec_allow = jnp.broadcast_to((key_ids < suffix_end)[None, :], (dec_count, key_count))
    dec_state = attend_blocks(states[1], dec_queries, key_rows, dec_allow)
    states = (tok_state, dec_state)
    whole_blocks = lax.all_gather(cache, "context", axis=1, tiled=True)
    slot_count = whole_blocks.shape[1]
    cache_key_rows = whole_blocks[0].reshape(slot_count * block_rows, kv_width)
    slot_keep = jnp.repeat(slot_live, block_rows)
    tok_allow = jnp.broadcast_to(slot_keep[None, :], (tok_count, slot_count * block_rows))
    tok_state = attend_blocks(states[0], queries, cache_key_rows, tok_allow)
    dec_allow = jnp.broadcast_to(slot_keep[None, :], (dec_count, slot_count * block_rows))
    dec_state = attend_blocks(states[1], dec_queries, cache_key_rows, dec_allow)
    states = (tok_state, dec_state)
    dec_state = states[1]
    dec_state = attend(dec_state, dec_queries, fresh, dec_ids[None, :] <= dec_ids[:, None])
    return (finish(states[0])[None], finish(dec_state)[None], fresh[None])


def solution(mesh):
    placed = (
        P("pool", "context", None, None),
        P("pool", None),
        P("pool"),
        P("pool"),
        P("pool", "context", None),
        P("pool", "context", "tensor", None),
        P("pool", None, None),
        P(("context", "tensor"), None),
        P(),
        P("pool", None, "tensor", None),
    )
    return jax.shard_map(
        on_device,
        mesh=mesh,
        in_specs=placed,
        out_specs=(
            P("pool", "context", "tensor", None),
            P("pool", None, "tensor", None),
            P("pool", None, None),
        ),
        check_vma=False,
    )
```

profile of v0, /device:TPU:0, one launch (start us, length us, event | category | flops | bytes accessed | tf_op | source)
XLA Modules:
  0.0 134.8 jit_solution(15165206399550961574)
XLA Ops:
  0.6 0.0 copy-start
  0.7 1.0 copy-done
  1.7 0.9 fusion.28
  2.6 35.4 %psum.7 = f32[2,576]{1,0:T(2,128)S(1)} all-reduce(f32[2,576]{1,0:T(2,128)S(1)} %fusion.28), channel_id=1, replica_groups=mesh['pool'=2,'context'=8,'tensor'=2] {'context','tensor'}, use_global_device_ids=true, to_apply=%region_9.10 | all-reduce | flops 1152 | bytes 9216 | tf_op jit(solution)/shard_map/psum | solution.py:110
  38.0 0.1 multiply_reduce_fusion
  38.2 0.8 multiply_convert_fusion
  40.2 0.1 fusion.38
  40.4 1.1 fusion.49
  41.5 0.7 fusion.22
  42.2 0.1 broadcast_in_dim.152
  42.3 0.1 broadcast_in_dim_reshape.4
  42.4 30.9 %all_gather.7 = bf16[1,8,16,576]{3,2,0,1:T(8,128)(2,1)S(1)} all-gather(bf16[1,1,16,576]{3,2,0,1:T(8,128)(2,1)} %bitcast.87), channel_id=1, replica_groups=mesh['pool'=2,'context'=8,'tensor'=2] {'context'}, dimensions={1}, use_global_device_ids=true | all-gather | bytes 165888 | tf_op jit(solution)/shard_map/all_gather | solution.py:131
  73.3 1.1 fusion.50
  74.5 31.9 %all_gather.6 = bf16[1,512,576]{2,1,0:T(8,128)(2,1)S(1)} all-gather(bf16[1,64,576]{2,1,0:T(8,128)(2,1)} %param.16), channel_id=1, replica_groups=mesh['pool'=2,'context'=8,'tensor'=2] {'context'}, dimensions={1}, use_global_device_ids=true | all-gather | bytes 663552 | tf_op jit(solution)/shard_map/all_gather | solution.py:116
  106.3 1.3 fusion.51
  107.6 0.2 convert_reduce_fusion.3
  107.8 0.1 convert_reduce_fusion.4
  107.9 0.2 convert_reduce_fusion.2
  108.1 0.2 fusion.17
  108.3 0.2 copy.34
  108.5 0.3 fusion.9
  108.8 0.8 fusion.12
  109.7 15.7 %conditional.1 = (f32[64,32]{1,0:T(8,128)}, f32[64,32]{1,0:T(8,128)S(1)}, f32[64,32,512]{2,1,0:T(8,128)}) conditional(s32[]{:T(128)} %convert_element_type.54, () %tuple.16, (s32[512]{0:T(512)S(1)}, s32[]{:T(128)}, s32[64]{0:T(128)S(1)}, bf16[64,32,576]{2,1,0:T(8,128)(2,1)}, bf16[512,576]{0,1:T(8,128)(2,1)S(1)}) %tuple.40), branch_computations={%region_0.0_spmd, %region_1.4_spmd} | conditional | flops 2298519552 | bytes 38456120 | solution.py:127
  109.7 0.1 broadcast_compare_fusion
  109.8 5.7 %fusion = (f32[64,32]{1,0:T(8,128)S(1)}, f32[64,32,512]{2,1,0:T(8,128)}) fusion(pred[64,512]{1,0:T(8,128)(4,1)S(1)} %broadcast_compare_fusion, bf16[64,32,576]{2,1,0:T(8,128)(2,1)} %get-tuple-element.15, bf16[512,576]{0,1:T(8,128)(2,1)S(1)} %get-tuple-element.45), kind=kOutput, calls=%fused_computation.3 | convolution fusion | flops 1211103232 | bytes 7184384 | tf_op jit(solution)/shard_map/cond/branch_1_fun/rhc,kc->rhk/dot_general | solution.py:16
  115.5 0.6 exponential_multiply_fusion
  116.1 0.3 copy.35
  116.4 0.0 copy-start.1
  116.4 5.9 %convolution_add_fusion = f32[64,32,512]{2,1,0:T(8,128)} fusion(f32[64,32]{1,0:T(8,128)S(1)} %get-tuple-element.46, bf16[512,576]{1,0:T(8,128)(2,1)S(1)} %copy.35, f32[64,32,512]{2,1,0:T(8,128)} %get-tuple-element.58, f32[64,32]{1,0:T(8,128)} %get-tuple-element.74, pred[64,512]{1,0:T(8,128)(4,1)S(1)} %broadcast_compare_fusion), kind=kOutput, calls=%fused_computation.4 | convolution fusion | flops 1080033280 | bytes 8986624 | tf_op jit(solution)/shard_map/cond/branch_1_fun/rhk,kc->rhc/dot_general | solution.py:25
  122.3 0.0 copy-done.1
  122.3 2.3 %convert_reduce_fusion = f32[64,32]{1,0:T(8,128)S(1)} fusion(f32[64,32]{1,0:T(8,128)} %get-tuple-element.74, f32[64,32,512]{2,1,0:T(8,128)S(1)} %copy-done.1, pred[64,512]{1,0:T(8,128)(4,1)S(1)} %broadcast_compare_fusion), kind=kLoop, calls=%fused_computation | loop fusion | flops 7337984 | bytes 4243456 | tf_op jit(solution)/shard_map/cond/branch_1_fun/reduce_sum | solution.py:24
  124.6 0.8 fusion.3
  125.4 2.7 %fusion.48 = (f32[64,32]{1,0:T(8,128)S(1)}, f32[64,32,128]{2,1,0:T(8,128)S(1)}) fusion(bf16[128,576,1]{1,0,2:T(8,128)(2,1)S(1)} %bitcast.85, bf16[1,64,32,576]{3,2,1,0:T(8,128)(2,1)} %param.17, pred[128]{0:T(512)(128)(4,1)S(1)} %broadcast_in_dim_reshape.4), kind=kOutput, calls=%fused_computation.93 | convolution fusion | flops 302774272 | bytes 3563648 | tf_op jit(solution)/shard_map/rhc,kc->rhk/dot_general | solution.py:16
  128.1 0.8 max.35
  128.9 0.6 convert_reduce_fusion.1
  129.5 0.8 multiply_add_fusion
  130.3 0.0 copy-start.2
  130.3 3.8 %fusion.4 = bf16[1,64,32,512]{3,2,1,0:T(8,128)(2,1)} fusion(f32[64,32]{1,0:T(8,128)S(1)} %get-tuple-element.55, f32[64,32,512]{2,1,0:T(8,128)} %get-tuple-element.23, f32[64,32]{1,0:T(8,128)S(1)} %get-tuple-element.56, bf16[128,576]{1,0:T(8,128)(2,1)S(1)} %bitcast.86, f32[64,32,128]{2,1,0:T(8,128)S(1)} %get-tuple-element.64, f32[64,32]{1,0:T(8,128)S(1)} %max.35, ...), kind=kOutput, calls=%fused_computation.14 | convolution fusion | flops 273416192 | bytes 7569920 | tf_op jit(solution)/shard_map/rhk,kc->rhc/dot_general | solution.py:25
  134.1 0.0 copy-done.2
  134.1 0.1 fusion.57
  134.2 0.7 pad_maximum_fusion
  (11 shorter events, 0.1 us)
Async XLA Ops:
  0.6 1.1 copy-start
  116.4 5.9 %copy-start.1 = (f32[64,32,512]{2,1,0:T(8,128)S(1)}, f32[64,32,512]{2,1,0:T(8,128)}, u32[]{:S(2)}) copy-start(f32[64,32,512]{2,1,0:T(8,128)} %get-tuple-element.58) | copy-start | bytes 12582916 | tf_op jit(solution)/shard_map/cond
  130.3 3.8 %copy-start.2 = (f32[512]{0:T(512)S(1)}, f32[512]{0:T(512)}, u32[]{:S(2)}) copy-start(f32[512]{0:T(512)} %param.20) | copy-start | bytes 6148
where the time goes:
time: 136 us; the launch traced here: 135 us
  blocking collectives  98.2 us (72%)
  matrix products  23.8 us (18%)
  other arithmetic  8.98 us (7%)
  between operations  2.06 us (2%)
  local copies, waits for them, and re-layouts  1.77 us (1%)
    psum x1, blocking collectives, on_device(): lax.psum(jnp.dot(hidden_part, kv_down, preferred_element_type=jnp.float32...  35.4 us
    all_gather x1, blocking collectives, on_device(): key_rows = lax.all_gather(suffix_latent, 'context', axis=1, tiled=True)[0]  31.9 us
    all_gather x1, blocking collectives, on_device(): whole_blocks = lax.all_gather(cache, 'context', axis=1, tiled=True)  30.9 us
    dot_general x5, matrix products, attend(): jnp.einsum('rhc,kc->rhk', queries, key_rows, preferred_element_type=jnp.f...  11.9 us
    dot_general x5, matrix products, attend(): jnp.einsum('rhk,kc->rhc', weights, key_rows[:, :lat_width], preferred_ele...  11 us
    reduce_sum x5, other arithmetic, attend(): jnp.sum(weights.astype(jnp.float32), axis=-1)  3.4 us

commit v1 on v0

v1 whole, which is shorter than its diff:
```python
import functools
import math

import jax
import jax.numpy as jnp
from jax import lax
from jax.experimental import pallas as pl
from jax.experimental.pallas import tpu as pltpu
from jax.sharding import PartitionSpec as P

SCALE = 192.0 ** (-0.5)
FACTOR = SCALE * 1.4426950408889634
NEG = -1e30
TILE = 16
LANES = 128
WIDE = 640
TAIL = 48
RADIX = 4
GROUPS = 16


def in_vmem(array):
    return pltpu.with_memory_space_constraint(array, pltpu.VMEM)


def in_hbm(array):
    return pltpu.with_memory_space_constraint(array, pltpu.HBM)


def dot(left, right):
    return jnp.dot(left, right, preferred_element_type=jnp.float32)


def score(keys, queries):
    return lax.dot_general(keys, queries, (((1,), (1,)), ((), ())), preferred_element_type=jnp.float32)


def pack_kernel(down_ref, hidden_ref, latent_ref, cache_ref, out_ref):
    core = lax.axis_index("tensor")
    down = down_ref[...]
    part, width = down.shape
    if hidden_ref.shape[1] == part:
        hidden = hidden_ref[...]
    else:
        pair = 2 * part
        start = pl.multiple_of(lax.axis_index("context") * pair, LANES)
        window = hidden_ref[:, pl.ds(start, pair)]
        hidden = jnp.where(core == 0, window[:, :part], window[:, part:])
    raw = dot(hidden, down)
    high = raw.astype(jnp.bfloat16).astype(jnp.float32)
    low = raw - high
    tok, cached = latent_ref.shape[1], cache_ref.shape[1]
    rows = tok + cached
    lat = width // LANES * LANES
    dec = raw.shape[0]
    for tile in range(2):
        at = pl.multiple_of(core * (lat // 2) + tile * LANES, LANES)
        out_ref[tile * rows : tile * rows + tok, :] = latent_ref[0, :, pl.ds(at, LANES)]
        out_ref[tile * rows + tok : (tile + 1) * rows, :] = cache_ref[0, :, pl.ds(at, LANES)]
    rope = jnp.concatenate(
        [latent_ref[0, :, lat:].astype(jnp.float32), cache_ref[0, :, lat:].astype(jnp.float32)], axis=0
    )
    left, right = split_rows(rows)
    rope = jnp.where(core == 0, rope[: rows // 2], rope[rows // 2 :])
    side = WIDE - width
    gap = jnp.zeros((left - right, side), jnp.float32)
    pieces = [jnp.concatenate([rope[:left], jnp.concatenate([rope[left:], gap], axis=0)], axis=1)]
    pieces += [piece[:, i : i + LANES] for piece in (high, low) for i in range(0, lat, LANES)]
    pieces.append(jnp.concatenate([high[:, lat:], low[:, lat:]], axis=1))
    used = sum(piece.shape[0] for piece in pieces)
    pieces.append(jnp.zeros((TAIL - used, LANES), jnp.float32))
    out_ref[2 * rows :, :] = jnp.concatenate(pieces, axis=0).astype(jnp.bfloat16)


def split_rows(rows):
    left = (rows // 4 + 7) // 8 * 8
    return left, rows // 2 - left


def stack_kernel(*refs):
    for i, ref in enumerate(refs[:-1]):
        refs[-1][i] = ref[...]


def fold(scores, values, state):
    top = jnp.max(scores, axis=0, keepdims=True)
    if state is not None:
        top = jnp.maximum(top, state[0])
    weights = jnp.exp2((scores - top) * FACTOR)
    whole = jnp.sum(weights, axis=0, keepdims=True)
    mixed = dot(values, weights.astype(jnp.bfloat16))
    if state is not None:
        fade = jnp.exp2((state[0] - top) * FACTOR)
        whole = whole + state[1] * fade
        mixed = mixed + state[2] * fade
    return top, whole, mixed


def ahead(order, begin, finish):
    started = begin(order[0])
    for block, following in zip(order, order[1:] + [None]):
        next_started = None if following is None else begin(following)
        finish(block, started)
        started = next_started


def read_state(mixed_ref, stat_ref, block, lanes, at=0):
    lanes = slice(at, at + lanes)
    return stat_ref[block, 0:1, lanes], stat_ref[block, 1:2, lanes], mixed_ref[block, :, lanes]


def write_state(mixed_ref, stat_ref, block, lanes, state):
    stat_ref[block, 0:1, :lanes] = state[0]
    stat_ref[block, 1:2, :lanes] = state[1]
    mixed_ref[block, :, :lanes] = state[2]


def table_kernel(shape, hits_ref, prefix_ref, length_ref, *refs):
    layout, tok, cached, block_rows = shape
    *table_refs, turn_ref = refs
    me = lax.axis_index("context")
    prefix = prefix_ref[0]
    length = length_ref[0]
    slots = cached // block_rows
    first = LANES - tok

    lane = lax.broadcasted_iota(jnp.int32, (tok, LANES), 1)
    bound = jnp.where(lane < first, length - 1, me * tok + lane - first)
    token = lax.broadcasted_iota(jnp.int32, (tok, LANES), 0)
    for keys, table_ref in zip(layout, table_refs):
        for i, key in enumerate(keys):
            source = me ^ key
            at = i * (tok + cached)
            allowed = token + source * tok <= bound
            table_ref[at : at + tok] = jnp.where(allowed, 0.0, NEG).astype(jnp.bfloat16)
            for slot in range(slots):
                live = jnp.int32(0)
                for b in range(hits_ref.shape[1]):
                    hit = jnp.logical_and(hits_ref[0, b] == source * slots + slot, b < prefix)
                    live = jnp.where(hit, 1, live)
                spot = at + tok + slot * block_rows
                mask = jnp.where(jnp.full((block_rows, LANES), live, jnp.int32) == 1, 0.0, NEG)
                table_ref[spot : spot + block_rows] = mask.astype(jnp.bfloat16)

    dec, rope = turn_ref.shape[1:]
    half = rope // 2
    step = lax.broadcasted_iota(jnp.int32, (dec, rope), 0)
    lane = lax.broadcasted_iota(jnp.int32, (dec, rope), 1)
    number = jnp.where(lane < half, lane, lane - half).astype(jnp.float32)
    position = (prefix * block_rows + length + step).astype(jnp.float32)
    angle = position * jnp.exp2(number * (-math.log2(10000.0) / half))
    turn_ref[0] = jnp.cos(angle)
    sine = jnp.sin(angle)
    turn_ref[1] = jnp.where(lane < half, -sine, sine)


def swap_halves(x):
    half = x.shape[1] // 2
    return jnp.concatenate([x[:, half:], x[:, :half]], axis=1)


def load_keys(keys_ref, pairs, table_ref, rows, side):
    core = lax.axis_index("tensor")
    left, right = split_rows(rows)
    in_key = lax.broadcasted_iota(jnp.int32, (rows, LANES), 1) < LANES - side
    at = 0
    for mine, theirs in pairs:
        halves = [jnp.where(core == 0, mine, theirs), jnp.where(core == 0, theirs, mine)]
        lane = 0
        tails = []
        for half in halves:
            for tile in range(2):
                keys_ref[at : at + rows, lane : lane + LANES] = half[tile * rows : (tile + 1) * rows]
                lane += LANES
            tail = half[2 * rows :].astype(jnp.float32)
            tails += [tail[:left], swap_halves(tail[:right])]
        rope = jnp.concatenate(tails, axis=0).astype(jnp.bfloat16)
        keys_ref[at : at + rows, lane:] = jnp.where(in_key, rope, table_ref[at : at + rows])
        at += rows


def middle_kernel(shape, marked_ref, decode_ref, table_ref, *refs):
    counts, rows, side, order, blocks, loaded = shape
    kinds = len(counts)
    if loaded:
        mixed_ref, stat_ref = refs[2:]
        keys, values = refs[0][...], refs[1][...]
        before = ()
    else:
        mixed_ref, stat_ref, keys_ref, values_ref = refs[-4:]
        own, other = refs[:kinds], refs[kinds : 2 * kinds]
        before = refs[2 * kinds : -4]
        pairs = [(mine[i], theirs[i]) for mine, theirs, n in zip(own, other, counts) for i in range(n)]
        load_keys(keys_ref, pairs, table_ref, rows, side)
        keys = keys_ref[...]
        values_ref[...] = keys_ref[:, : values_ref.shape[0]].T
        values = values_ref[...]
    lanes_all = mixed_ref.shape[2]

    def lanes_of(index):
        return LANES if order[index] == blocks - 1 else lanes_all

    def begin(index):
        if order[index] == blocks - 1:
            return score(keys, decode_ref[...]) + table_ref[...].astype(jnp.float32)
        return score(keys, marked_ref[index])

    def finish(index, scores):
        lanes = lanes_of(index)
        state = read_state(*before, index, lanes) if before else None
        write_state(mixed_ref, stat_ref, index, lanes, fold(scores, values, state))

    ahead(list(range(len(order))), begin, finish)


def last_kernel(
    shape, marked_ref, late_ref, decode_ref, table_ref, turn_ref, gain_ref, *refs
):
    counts, rows, heads, dec, width = shape
    kinds = len(counts)
    own, other = refs[:kinds], refs[kinds : 2 * kinds]
    states = [refs[2 * kinds : 2 * kinds + 2], refs[2 * kinds + 2 : 2 * kinds + 4]]
    out_hbm, decode_hbm, fresh_hbm = refs[2 * kinds + 4 : 2 * kinds + 7]
    keys_ref, out_ref, decode_out_ref, fresh_ref, sem = refs[2 * kinds + 7 :]
    cut, lat, lanes_all = states[0][0].shape
    blocks = cut + states[1][0].shape[0]
    steps = blocks - 1
    groups = lanes_all // heads
    side = WIDE - width

    def store(block, half):
        size = groups // 2
        return pltpu.make_async_copy(
            out_ref.at[block, pl.ds(half * size, size)],
            out_hbm.at[0, pl.ds(block * groups + half * size, size)],
            sem.at[block, half],
        )

    decode_store = pltpu.make_async_copy(decode_out_ref, decode_hbm, sem.at[steps, 0])
    fresh_store = pltpu.make_async_copy(fresh_ref, fresh_hbm, sem.at[steps, 1])

    pairs = [(own[-1][i], other[-1][i]) for i in range(counts[-1])]
    load_keys(keys_ref, pairs, table_ref, rows, side)
    values = keys_ref[:, :lat].T

    def fresh_keys():
        sums = None
        for ref, count in zip(own + other, counts + counts):
            for i in range(count):
                part = ref[i, 2 * rows :, :].astype(jnp.float32)
                sums = part if sums is None else sums + part
        at = split_rows(rows)[0]
        pieces = [sums[at + i * dec : at + (i + 1) * dec] for i in range(2 * lat // LANES + 1)]
        tiles = lat // LANES
        raw = [pieces[i] + pieces[tiles + i] for i in range(tiles)]
        rope = pieces[-1][:, :side] + pieces[-1][:, side:]
        latent = jnp.concatenate(raw, axis=1)
        mean = jnp.sum(latent * latent, axis=-1, keepdims=True) * (1.0 / lat)
        normed = latent * lax.rsqrt(mean + 1e-06) * gain_ref[...]
        rotated = rope * turn_ref[0] + swap_halves(rope) * turn_ref[1]
        fresh = jnp.concatenate([normed, rotated], axis=1)
        fresh_ref[0] = fresh.astype(jnp.bfloat16)
        fresh = jnp.concatenate([fresh, jnp.zeros((dec, side), jnp.float32)], axis=1)
        fresh = jnp.concatenate([fresh, jnp.zeros((TILE - dec, WIDE), jnp.float32)], axis=0)
        row = lax.broadcasted_iota(jnp.int32, (TILE, LANES), 0)
        lane = lax.broadcasted_iota(jnp.int32, (TILE, LANES), 1)
        shift = jnp.where(row <= lax.div(lane, heads), 0.0, NEG)
        return fresh.astype(jnp.bfloat16), jnp.where(row < dec, shift, NEG)

    fresh, fresh_shift = fresh_keys()
    fresh_store.start()

    def begin(block):
        if block == steps:
            return score(keys_ref[...], decode_ref[...]) + table_ref[...].astype(jnp.float32)
        return score(keys_ref[...], marked_ref[block] if block < cut else late_ref[block - cut])

    def finish(block, scores):
        half, index = (0, block) if block < cut else (1, block - cut)
        last = block == steps
        state = read_state(*states[half], index, LANES if last else lanes_all)
        state = fold(scores, values, state)
        if last:
            state = fold(score(fresh, decode_ref[...]) + fresh_shift, fresh[:, :lat].T, state)
        scale = 1.0 / state[1]
        if last:
            result = (state[2] * scale).astype(jnp.bfloat16).T
            decode_out_ref[0] = result[: dec * heads].reshape(dec, heads, lat)
            decode_store.start()
            return
        for half in range(2):
            some = slice(half * lanes_all // 2, (half + 1) * lanes_all // 2)
            result = (state[2][:, some] * scale[:, some]).astype(jnp.bfloat16).T
            out_ref[block, pl.ds(half * (groups // 2), groups // 2)] = result.reshape(-1, heads, lat)
            store(block, half).start()

    ahead([*range(steps - 1), steps, steps - 1], begin, finish)
    for block in range(steps):
        for half in range(2):
            store(block, half).wait()
    decode_store.wait()
    fresh_store.wait()


def on_device(
    cache,
    hit_slots,
    prefix_blocks,
    suffix_len,
    suffix_latent,
    suffix_query,
    decode_hidden,
    kv_down,
    kv_gain,
    decode_query,
    count,
):
    lat = kv_gain.shape[0]
    own_slots, block_rows, width = cache.shape[1:]
    cached = own_slots * block_rows
    tok = suffix_latent.shape[1]
    dec, heads = decode_query.shape[1:3]
    radix = math.gcd(count, RADIX)
    pages = count // radix
    vmem = pl.BlockSpec(memory_space=pltpu.VMEM)
    smem = pl.BlockSpec(memory_space=pltpu.SMEM)
    anywhere = pl.BlockSpec(memory_space=pl.ANY)
    small = pltpu.CompilerParams(vmem_limit_bytes=8 << 20)
    large = pltpu.CompilerParams(vmem_limit_bytes=24 << 20)

    part = kv_down.shape[0]
    hidden = decode_hidden[0]
    if 2 * part % LANES:
        part_index = lax.axis_index(("context", "tensor"))
        hidden = lax.dynamic_slice_in_dim(hidden, part_index * part, part, 1)
    block = tok + cached
    rows = 2 * block + TAIL
    message = pl.pallas_call(
        pack_kernel,
        out_shape=pltpu.VMEM((rows, LANES), jnp.bfloat16),
        in_specs=[vmem] * 4,
        out_specs=vmem,
        compiler_params=small,
    )(in_hbm(kv_down), in_hbm(hidden), in_hbm(suffix_latent), in_hbm(cache.reshape(1, cached, width)))

    def send(array, hop):
        return lax.ppermute(array, "context", [(rank, rank ^ hop) for rank in range(count)])

    def swap(array):
        return lax.ppermute(array, "tensor", [(0, 1), (1, 0)])

    def stack(*arrays):
        return pl.pallas_call(
            stack_kernel,
            out_shape=pltpu.VMEM((len(arrays), rows, LANES), jnp.bfloat16),
            in_specs=[vmem] * len(arrays),
            out_specs=vmem,
            compiler_params=small,
        )(*arrays)

    hops = list(range(1, pages))
    leaps = [digit * pages for digit in range(1, radix)]
    layout = [[0, *hops, *leaps]] + [[leap + hop for leap in leaps] for hop in hops]
    beside = [send(message, hop) for hop in hops]
    across = [send(message, leap) for leap in leaps]

    groups = math.gcd(tok, GROUPS)
    steps = tok // groups
    lanes = groups * heads
    blocks = steps + 1

    *tables, turn = pl.pallas_call(
        functools.partial(table_kernel, (layout, tok, cached, block_rows)),
        out_shape=tuple(pltpu.VMEM((len(keys) * block, LANES), jnp.bfloat16) for keys in layout)
        + (pltpu.VMEM((2, dec, width - lat), jnp.float32),),
        in_specs=[smem, smem, smem],
        out_specs=(vmem,) * (len(layout) + 1),
        compiler_params=small,
    )(in_hbm(hit_slots), prefix_blocks, suffix_len)

    def mark(query, begin, end):
        part = query[0, begin * groups : end * groups]
        shape = part.shape[:2] + (WIDE - width,)
        owner = lax.broadcasted_iota(jnp.int32, shape, 0) + begin * groups
        hot = (owner == lax.broadcasted_iota(jnp.int32, shape, 2)).astype(jnp.bfloat16)
        return jnp.concatenate([part, hot], axis=2).reshape(end - begin, lanes, WIDE)

    decode_rows = jnp.pad(
        decode_query.reshape(dec * heads, width), ((0, LANES - dec * heads), (0, WIDE - width))
    )

    held = lax.optimization_barrier((turn, *tables, *beside, *across))
    turn, tables, held = held[0], held[1 : 1 + pages], held[1 + pages :]
    beside, across = held[: pages - 1], held[pages - 1 :]
    far = stack(*across)
    ends = [send(far, hop) for hop in hops]
    own = [stack(message, *beside), far]
    other = [swap(array) for array in own]
    early, far = lax.optimization_barrier((suffix_query, far))
    marked = mark(early, 0, steps - 1)

    def middle(marked, table, own, other, order, *state, loaded=()):
        counts = [array.shape[0] for array in own]
        size = sum(counts) * block
        inputs = [in_vmem(marked), in_vmem(decode_rows), table, *(loaded or (*own, *other)), *state]
        aliases = {len(inputs) - 2: 0, len(inputs) - 1: 1} if state else {}
        kept = () if loaded else ((size, WIDE), (lat, size))
        return pl.pallas_call(
            functools.partial(
                middle_kernel, (counts, block, WIDE - width, order, blocks, bool(loaded))
            ),
            out_shape=(
                pltpu.VMEM((len(order), lat, lanes), jnp.float32),
                pltpu.VMEM((len(order), 8, lanes), jnp.float32),
                *(pltpu.VMEM(shape, jnp.bfloat16) for shape in kept),
            ),
            in_specs=[vmem] * len(inputs),
            out_specs=(vmem,) * (2 + len(kept)),
            input_output_aliases=aliases,
            compiler_params=large,
        )(*inputs)

    orders = list(range(blocks - 2)), [blocks - 2, blocks - 1]
    mixed, stat, *loaded = middle(marked, tables[0], own, other, orders[0])
    later, stat = lax.optimization_barrier((suffix_query, stat))
    late = mark(later, steps - 1, steps)
    mixed, stat, late, decode_rows, *ends = lax.optimization_barrier(
        (mixed, stat, late, decode_rows, *ends)
    )
    states = [
        (mixed, stat),
        middle(late, tables[0], own, other, orders[1], loaded=loaded)[:2],
    ]
    own += ends
    other += [swap(array) for array in ends]
    for number in range(1, pages - 1):
        chosen = slice(1 + number, 2 + number)
        states = [
            middle(part, tables[number], own[chosen], other[chosen], order, *state)[:2]
            for part, order, state in zip((marked, late), orders, states)
        ]
    counts = [array.shape[0] for array in own]
    return pl.pallas_call(
        functools.partial(last_kernel, (counts, block, heads, dec, width)),
        out_shape=(
            jax.ShapeDtypeStruct((1, tok, heads, lat), jnp.bfloat16),
            jax.ShapeDtypeStruct((1, dec, heads, lat), jnp.bfloat16),
            jax.ShapeDtypeStruct((1, dec, width), jnp.bfloat16),
        ),
        in_specs=[vmem] * (10 + 2 * len(own)),
        out_specs=(anywhere,) * 3,
        scratch_shapes=[
            pltpu.VMEM((counts[-1] * block, WIDE), jnp.bfloat16),
            pltpu.VMEM((steps, groups, heads, lat), jnp.bfloat16),
            pltpu.VMEM((1, dec, heads, lat), jnp.bfloat16),
            pltpu.VMEM((1, dec, width), jnp.bfloat16),
            pltpu.SemaphoreType.DMA((blocks, 2)),
        ],
        compiler_params=large,
    )(in_vmem(marked), in_vmem(late), in_vmem(decode_rows), tables[-1], turn, in_hbm(kv_gain.reshape(1, lat)), *own, *other, *states[0], *states[1])


def solution(mesh):
    placed = (
        P("pool", "context", None, None),
        P("pool", None),
        P("pool"),
        P("pool"),
        P("pool", "context", None),
        P("pool", "context", "tensor", None),
        P("pool", None, None),
        P(("context", "tensor"), None),
        P(),
        P("pool", None, "tensor", None),
    )
    return jax.shard_map(
        functools.partial(on_device, count=mesh.shape["context"]),
        mesh=mesh,
        in_specs=placed,
        out_specs=(
            P("pool", "context", "tensor", None),
            P("pool", None, "tensor", None),
            P("pool", None, None),
        ),
        check_vma=False,
    )
```

time: 136 us -> 24.2 us (0.18)
  blocking collectives: 98.2 us -> 0 us
  matrix products: 23.8 us -> 0 us
  Pallas kernels: 0 us -> 9.73 us
  starting transfers between devices: 0 us -> 8.61 us
  other arithmetic: 8.98 us -> 0.81 us
    all_gather x2 -> x0, blocking collectives: 62.7 us -> none  [the longest x1 31.9 us: on_device(): key_rows = lax.all_gather(suffix_latent, 'context', axis=1, tiled=True)[0]]
    psum x1 -> x0, blocking collectives: 35.4 us -> none  [on_device(): lax.psum(jnp.dot(hidden_part, kv_down, preferred_element_type=jnp.float32...]
    dot_general x11 -> x0, matrix products: 23.8 us -> none  [the longest x5 11.9 us: attend(): jnp.einsum('rhc,kc->rhk', queries, key_rows, preferred_element_type=jnp.f...]
    pallas_call x0 -> x7, Pallas kernels: none -> 9.73 us  [the longest x1 3.97 us: on_device(): pl.pallas_call(functools.partial(last_kernel, (counts, block, heads, dec,...]
    ppermute x0 -> x8, starting transfers between devices: none -> 8.61 us  [the longest x5 7.95 us: send(): lax.ppermute(array, 'context', [(rank, rank ^ hop) for rank in range(coun...]
    reduce_sum x6 -> x0, other arithmetic: 3.52 us -> none  [the longest x5 3.4 us: attend(): jnp.sum(weights.astype(jnp.float32), axis=-1)]
    add x4 -> x1, other arithmetic: 1.58 us -> 0.01 us  [mark(): owner = lax.broadcasted_iota(jnp.int32, shape, 0) + begin * groups]
  transfers between devices with their start and end apart: 0 -> 8, of which waited for: 0 -> 1; matrix products, arithmetic and copies ran while one was open for 0% -> 8% of each run, Pallas kernels for 0% -> 18%
where the time goes in v1:
time: 24.2 us; the launch traced here: 23.9 us
  Pallas kernels  9.73 us (40%)
  starting transfers between devices  8.61 us (36%)
  local copies, waits for them, and re-layouts  2.19 us (9%)
  between operations  2.07 us (9%)
  other arithmetic  0.81 us (3%)
  waiting for transfers between devices  0.52 us (2%)
    ppermute x5, starting transfers between devices, send(): lax.ppermute(array, 'context', [(rank, rank ^ hop) for rank in range(coun...  7.95 us
    pallas_call x1, Pallas kernels, on_device(): pl.pallas_call(functools.partial(last_kernel, (counts, block, heads, dec,...  3.97 us
    pallas_call x2, Pallas kernels, middle(): pl.pallas_call(functools.partial(middle_kernel, (counts, block, WIDE - wi...  3.6 us
    pallas_call x1, Pallas kernels, on_device(): pl.pallas_call(pack_kernel, out_shape=pltpu.VMEM((rows, LANES), jnp.bfloa...  1.4 us
    slice x4, local copies, waits for them, and re-layouts, mark(): part = query[0, begin * groups:end * groups]  0.98 us
    pad x1, local copies, waits for them, and re-layouts, on_device(): jnp.pad(decode_query.reshape(dec * heads, width), ((0, LANES - dec * head...  0.9 us
    pallas_call x1, Pallas kernels, on_device(): pl.pallas_call(functools.partial(table_kernel, (layout, tok, cached, bloc...  0.74 us
    ppermute x3, starting transfers between devices, swap(): return lax.ppermute(array, 'tensor', [(0, 1), (1, 0)])  0.66 us
  transfers between devices with their start and end apart: 8, of which 1 were waited for; matrix products, arithmetic and copies ran while one was open for 8% of the time, Pallas kernels for 18%

profile of v1, /device:TPU:0, one launch (start us, length us, event | category | flops | bytes accessed | tf_op | source)
XLA Modules:
  0.0 23.9 jit_solution(15384990534405832340)
XLA Ops:
  0.6 1.4 %shard_map.122.refs_0_ = bf16[208,128]{1,0:T(8,128)(2,1)S(1)} custom-call(bf16[448,576]{1,0:T(8,128)(2,1)} %down_ref.1, bf16[2,7168]{1,0:T(2,128)(2,1)} %bitcast.9, bf16[1,64,576]{2,1,0:T(8,128)(2,1)} %latent_ref.1, bf16[1,16,576]{2,1,0:T(8,128)(2,1)} %bitcast.10), custom_call_target="tpu_custom_call" | custom-call | tf_op jit(solution)/shard_map/pallas_call | solution.py:338
  2.0 5.1 %collective-permute-start.3 = (bf16[208,128]{1,0:T(8,128)(2,1)S(1)}, bf16[208,128]{1,0:T(8,128)(2,1)S(1)}, u32[]{:S(2)}, u32[]{:S(2)}) collective-permute-start(bf16[208,128]{1,0:T(8,128)(2,1)S(1)} %shard_map.122.refs_0_), channel_id=1, source_target_pairs={{0,12},{2,14},{4,8},{6,10},{8,4},{10,6},{12,0},{14,2},{1,13},{3,15... | collective-permute-start | bytes 159752 | tf_op jit(solution)/shard_map/ppermute | solution.py:347
  7.1 0.0 collective-permute-start.2
  7.1 0.6 %collective-permute-start.1 = (bf16[208,128]{1,0:T(8,128)(2,1)S(1)}, bf16[208,128]{1,0:T(8,128)(2,1)S(1)}, u32[]{:S(2)}, u32[]{:S(2)}) collective-permute-start(bf16[208,128]{1,0:T(8,128)(2,1)S(1)} %shard_map.122.refs_0_), channel_id=1, source_target_pairs={{0,4},{2,6},{4,0},{6,2},{8,12},{10,14},{12,8},{14,10},{1,5},{3,7},... | collective-permute-start | bytes 159752 | tf_op jit(solution)/shard_map/ppermute | solution.py:347
  7.7 1.7 %collective-permute-start = (bf16[208,128]{1,0:T(8,128)(2,1)S(1)}, bf16[208,128]{1,0:T(8,128)(2,1)S(1)}, u32[]{:S(2)}, u32[]{:S(2)}) collective-permute-start(bf16[208,128]{1,0:T(8,128)(2,1)S(1)} %shard_map.122.refs_0_), channel_id=1, source_target_pairs={{0,2},{2,0},{4,6},{6,4},{8,10},{10,8},{12,14},{14,12},{1,3},{3,1},... | collective-permute-start | bytes 159752 | tf_op jit(solution)/shard_map/ppermute | solution.py:347
  9.4 0.1 iota.54
  9.5 0.1 iota.55
  9.6 0.1 iota.49
  9.6 0.1 iota.50
  9.7 0.3 %fusion = bf16[3,512,64]{2,1,0:T(8,128)(2,1)S(1)} fusion(s32[3,512]{1,0:T(4,128)S(1)} %iota.50), kind=kLoop, calls=%fused_computation.2 | loop fusion | flops 196608 | bytes 202752 | tf_op jit(solution)/shard_map/convert_element_type | solution.py:385
  10.0 0.1 fusion.1
  11.4 0.9 %pad.4.decode_ref = bf16[128,640]{1,0:T(8,128)(2,1)S(1)} pad(bf16[64,576]{1,0:T(8,128)(2,1)} %bitcast.8, bf16[]{:T(256)} %constant.5.clone.1), padding=0_64x0_64 | pad | bytes 237570 | tf_op jit(solution)/shard_map/jit(_pad)/pad | solution.py:388
  12.3 0.7 %shard_map.121 = (bf16[400,128]{1,0:T(8,128)(2,1)S(1)}, bf16[240,128]{1,0:T(8,128)(2,1)S(1)}, f32[2,2,64]{2,1,0:T(2,128)S(1)}) custom-call(s32[1,8]{1,0:T(1,128)} %hits_ref.1, s32[1]{0:T(128)S(6)} %copy.13.prefix_ref, s32[1]{0:T(128)S(6)} %copy.14.length_ref), custom_call_target="tpu_custom_call" | custom-call | tf_op jit(solution)/shard_map/pallas_call | solution.py:372
  13.1 0.0 collective-permute-done.3.refs_2_
  13.1 0.0 collective-permute-done.2.refs_1_
  13.1 0.0 collective-permute-done.1.refs_0_
  13.1 0.0 collective-permute-done.refs_1_
  13.1 0.6 %collective-permute-start.6 = (bf16[3,208,128]{2,1,0:T(8,128)(2,1)S(1)}, bf16[3,208,128]{2,1,0:T(8,128)(2,1)S(1)}, u32[]{:S(2)}, u32[]{:S(2)}) collective-permute-start(bf16[3,208,128]{2,1,0:T(8,128)(2,1)S(1)} %shard_map.123.refs_1_), channel_id=1, source_target_pairs={{0,2},{2,0},{4,6},{6,4},{8,10},{10,8},{12,14},{14,12},{1,3},{3,1},... | collective-permute-start | bytes 479240 | tf_op jit(solution)/shard_map/ppermute | solution.py:347
  13.7 0.0 collective-permute-start.5
  13.7 0.0 slice-start
  13.8 0.6 %collective-permute-start.4 = (bf16[2,208,128]{2,1,0:T(8,128)(2,1)S(1)}, bf16[2,208,128]{2,1,0:T(8,128)(2,1)S(1)}, u32[]{:S(2)}, u32[]{:S(2)}) collective-permute-start(bf16[2,208,128]{2,1,0:T(8,128)(2,1)S(1)} %shard_map.124.refs_0_), channel_id=1, source_target_pairs={{0,1},{1,0},{2,3},{3,2},{4,5},{5,4},{6,7},{7,6},{8,9},{9,8},{10,11... | collective-permute-start | bytes 319496 | tf_op jit(solution)/shard_map/ppermute | solution.py:350
  14.3 1.0 %slice-done = bf16[1,48,32,576]{3,2,1,0:T(8,128)(2,1)S(1)} async-done(((bf16[1,64,32,576]{3,2,1,0:T(8,128)(2,1)}), bf16[1,48,32,576]{3,2,1,0:T(8,128)(2,1)S(1)}, s32[]{:S(2)}) %slice-start) | async-done | bytes 1769496 | tf_op jit(solution)/shard_map/slice | solution.py:382
  15.3 0.3 %pad_maximum_fusion.marked_ref = bf16[3,512,640]{2,1,0:T(8,128)(2,1)S(1)} fusion(bf16[3,512,64]{2,1,0:T(8,128)(2,1)S(1)} %fusion, bf16[3,512,576]{2,1,0:T(8,128)(2,1)S(1)} %bitcast.6), kind=kLoop, calls=%fused_computation | loop fusion | flops 3932160 | bytes 3932160 | tf_op jit(solution)/shard_map/concatenate | solution.py:386
  15.6 0.0 slice-start.1
  15.6 0.0 collective-permute-done.4.refs_2_.refs_3_
  15.6 0.0 collective-permute-done.5.refs_3_.refs_4_
  15.6 2.2 %shard_map.125 = (f32[3,512,512]{2,1,0:T(8,128)S(1)}, f32[3,8,512]{2,1,0:T(8,128)S(1)}, bf16[400,640]{1,0:T(8,128)(2,1)S(1)}, bf16[512,400]{1,0:T(8,128)(2,1)S(1)}) custom-call(bf16[3,512,640]{2,1,0:T(8,128)(2,1)S(1)} %pad_maximum_fusion.marked_ref, bf16[128,640]{1,0:T(8,128)(2,1)S(1)} %pad.4.decode_ref, bf16[400,128]{1,0:T(8,128)(2,1)S(1)} %get-tuple-element.34.table_ref, ...), custom_call_target="tpu_custom_call" | custom-call | tf_op jit(solution)/shard_map/pallas_call | solution.py:408
  17.9 0.0 slice-done.1
  17.9 0.1 pad_maximum_fusion.1.marked_ref.late_ref
  18.0 0.5 %collective-permute-done.6.refs_2_ = bf16[3,208,128]{2,1,0:T(8,128)(2,1)S(1)} collective-permute-done((bf16[3,208,128]{2,1,0:T(8,128)(2,1)S(1)}, bf16[3,208,128]{2,1,0:T(8,128)(2,1)S(1)}, u32[]{:S(2)}, u32[]{:S(2)}) %collective-permute-start.6) | collective-permute-done | bytes 159776 | tf_op jit(solution)/shard_map/ppermute | solution.py:347
  18.5 0.1 collective-permute-start.7
  18.6 1.4 %shard_map.126 = (f32[2,512,512]{2,1,0:T(8,128)S(1)}, f32[2,8,512]{2,1,0:T(8,128)S(1)}) custom-call(bf16[1,512,640]{2,1,0:T(8,128)(2,1)S(1)} %pad_maximum_fusion.1.marked_ref.late_ref, bf16[128,640]{1,0:T(8,128)(2,1)S(1)} %pad.4.decode_ref, bf16[400,128]{1,0:T(8,128)(2,1)S(1)} %get-tuple-element.34.table_ref, ...), custom_call_target="tpu_custom_call" | custom-call | tf_op jit(solution)/shard_map/pallas_call | solution.py:408
  19.9 0.0 collective-permute-done.7.refs_5_
  20.0 4.0 %shard_map.127 = (bf16[1,64,32,512]{3,2,1,0:T(8,128)(2,1)}, bf16[1,2,32,512]{3,2,1,0:T(8,128)(2,1)}, bf16[1,2,576]{2,1,0:T(2,128)(2,1)}) custom-call(bf16[3,512,640]{2,1,0:T(8,128)(2,1)S(1)} %pad_maximum_fusion.marked_ref, bf16[1,512,640]{2,1,0:T(8,128)(2,1)S(1)} %pad_maximum_fusion.1.marked_ref.late_ref, bf16[128,640]{1,0:T(8,128)(2,1)S(1)} %pad.4.decode_ref, ...), custom_call_target="tpu_custom_call" | custom-call | tf_op jit(solution)/shard_map/pallas_call | solution.py:443
  (4 shorter events, 0.0 us)
Async XLA Ops:
  2.0 11.1 %collective-permute-start.3 = (bf16[208,128]{1,0:T(8,128)(2,1)S(1)}, bf16[208,128]{1,0:T(8,128)(2,1)S(1)}, u32[]{:S(2)}, u32[]{:S(2)}) collective-permute-start(bf16[208,128]{1,0:T(8,128)(2,1)S(1)} %shard_map.122.refs_0_), channel_id=1, source_target_pairs={{0,12},{2,14},{4,8},{6,10},{8,4},{10,6},{12,0},{14,2},{1,13},{3,15... | collective-permute-start | bytes 159752 | tf_op jit(solution)/shard_map/ppermute | solution.py:347
  7.1 6.0 %collective-permute-start.2 = (bf16[208,128]{1,0:T(8,128)(2,1)S(1)}, bf16[208,128]{1,0:T(8,128)(2,1)S(1)}, u32[]{:S(2)}, u32[]{:S(2)}) collective-permute-start(bf16[208,128]{1,0:T(8,128)(2,1)S(1)} %shard_map.122.refs_0_), channel_id=1, source_target_pairs={{0,8},{2,10},{4,12},{6,14},{8,0},{10,2},{12,4},{14,6},{1,9},{3,11}... | collective-permute-start | bytes 159752 | tf_op jit(solution)/shard_map/ppermute | solution.py:347
  7.1 6.0 %collective-permute-start.1 = (bf16[208,128]{1,0:T(8,128)(2,1)S(1)}, bf16[208,128]{1,0:T(8,128)(2,1)S(1)}, u32[]{:S(2)}, u32[]{:S(2)}) collective-permute-start(bf16[208,128]{1,0:T(8,128)(2,1)S(1)} %shard_map.122.refs_0_), channel_id=1, source_target_pairs={{0,4},{2,6},{4,0},{6,2},{8,12},{10,14},{12,8},{14,10},{1,5},{3,7},... | collective-permute-start | bytes 159752 | tf_op jit(solution)/shard_map/ppermute | solution.py:347
  7.7 5.4 %collective-permute-start = (bf16[208,128]{1,0:T(8,128)(2,1)S(1)}, bf16[208,128]{1,0:T(8,128)(2,1)S(1)}, u32[]{:S(2)}, u32[]{:S(2)}) collective-permute-start(bf16[208,128]{1,0:T(8,128)(2,1)S(1)} %shard_map.122.refs_0_), channel_id=1, source_target_pairs={{0,2},{2,0},{4,6},{6,4},{8,10},{10,8},{12,14},{14,12},{1,3},{3,1},... | collective-permute-start | bytes 159752 | tf_op jit(solution)/shard_map/ppermute | solution.py:347
  13.1 5.3 %collective-permute-start.6 = (bf16[3,208,128]{2,1,0:T(8,128)(2,1)S(1)}, bf16[3,208,128]{2,1,0:T(8,128)(2,1)S(1)}, u32[]{:S(2)}, u32[]{:S(2)}) collective-permute-start(bf16[3,208,128]{2,1,0:T(8,128)(2,1)S(1)} %shard_map.123.refs_1_), channel_id=1, source_target_pairs={{0,2},{2,0},{4,6},{6,4},{8,10},{10,8},{12,14},{14,12},{1,3},{3,1},... | collective-permute-start | bytes 479240 | tf_op jit(solution)/shard_map/ppermute | solution.py:347
  13.7 1.9 %collective-permute-start.5 = (bf16[3,208,128]{2,1,0:T(8,128)(2,1)S(1)}, bf16[3,208,128]{2,1,0:T(8,128)(2,1)S(1)}, u32[]{:S(2)}, u32[]{:S(2)}) collective-permute-start(bf16[3,208,128]{2,1,0:T(8,128)(2,1)S(1)} %shard_map.123.refs_1_), channel_id=1, source_target_pairs={{0,1},{1,0},{2,3},{3,2},{4,5},{5,4},{6,7},{7,6},{8,9},{9,8},{10,11... | collective-permute-start | bytes 479240 | tf_op jit(solution)/shard_map/ppermute | solution.py:350
  13.7 1.5 %slice-start = ((bf16[1,64,32,576]{3,2,1,0:T(8,128)(2,1)}), bf16[1,48,32,576]{3,2,1,0:T(8,128)(2,1)S(1)}, s32[]{:S(2)}) async-start(bf16[1,64,32,576]{3,2,1,0:T(8,128)(2,1)} %param.15), calls=%async_computation | async-start | bytes 3932160 | tf_op jit(solution)/shard_map/slice | solution.py:382
  13.8 1.8 %collective-permute-start.4 = (bf16[2,208,128]{2,1,0:T(8,128)(2,1)S(1)}, bf16[2,208,128]{2,1,0:T(8,128)(2,1)S(1)}, u32[]{:S(2)}, u32[]{:S(2)}) collective-permute-start(bf16[2,208,128]{2,1,0:T(8,128)(2,1)S(1)} %shard_map.124.refs_0_), channel_id=1, source_target_pairs={{0,1},{1,0},{2,3},{3,2},{4,5},{5,4},{6,7},{7,6},{8,9},{9,8},{10,11... | collective-permute-start | bytes 319496 | tf_op jit(solution)/shard_map/ppermute | solution.py:350
  15.6 2.3 %slice-start.1 = ((bf16[1,64,32,576]{3,2,1,0:T(8,128)(2,1)}), bf16[1,16,32,576]{3,2,1,0:T(8,128)(2,1)S(1)}, s32[]{:S(2)}) async-start(bf16[1,64,32,576]{3,2,1,0:T(8,128)(2,1)} %param.15), calls=%async_computation.1 | async-start | bytes 1310720 | tf_op jit(solution)/shard_map/slice | solution.py:382
  18.5 1.5 %collective-permute-start.7 = (bf16[3,208,128]{2,1,0:T(8,128)(2,1)S(1)}, bf16[3,208,128]{2,1,0:T(8,128)(2,1)S(1)}, u32[]{:S(2)}, u32[]{:S(2)}) collective-permute-start(bf16[3,208,128]{2,1,0:T(8,128)(2,1)S(1)} %collective-permute-done.6.refs_2_), channel_id=1, source_target_pairs={{0,1},{1,0},{2,3},{3,2},{4,5},{5,4},{6,7},{7,6},{8,9},{9,8},{10,11... | collective-permute-start | bytes 479240 | tf_op jit(solution)/shard_map/ppermute | solution.py:350

commit v2 on v1

--- a/solution.py
+++ b/solution.py
@@ -117,7 +117,10 @@
 
 def table_kernel(shape, hits_ref, prefix_ref, length_ref, *refs):
     layout, tok, cached, block_rows = shape
-    *table_refs, turn_ref = refs
+    *table_refs, turn_ref, hot_ref = refs
+    token = lax.broadcasted_iota(jnp.int32, hot_ref.shape, 0)
+    hot = token == lax.broadcasted_iota(jnp.int32, hot_ref.shape, 2)
+    hot_ref[...] = jnp.where(hot, 1.0, 0.0).astype(jnp.bfloat16)
     me = lax.axis_index("context")
     prefix = prefix_ref[0]
     length = length_ref[0]
@@ -369,39 +372,36 @@
     lanes = groups * heads
     blocks = steps + 1
 
-    *tables, turn = pl.pallas_call(
+    *tables, turn, hot = pl.pallas_call(
         functools.partial(table_kernel, (layout, tok, cached, block_rows)),
         out_shape=tuple(pltpu.VMEM((len(keys) * block, LANES), jnp.bfloat16) for keys in layout)
-        + (pltpu.VMEM((2, dec, width - lat), jnp.float32),),
+        + (
+            pltpu.VMEM((2, dec, width - lat), jnp.float32),
+            pltpu.VMEM((tok, heads, WIDE - width), jnp.bfloat16),
+        ),
         in_specs=[smem, smem, smem],
-        out_specs=(vmem,) * (len(layout) + 1),
+        out_specs=(vmem,) * (len(layout) + 2),
         compiler_params=small,
     )(in_hbm(hit_slots), prefix_blocks, suffix_len)
 
     def mark(query, begin, end):
-        part = query[0, begin * groups : end * groups]
-        shape = part.shape[:2] + (WIDE - width,)
-        owner = lax.broadcasted_iota(jnp.int32, shape, 0) + begin * groups
-        hot = (owner == lax.broadcasted_iota(jnp.int32, shape, 2)).astype(jnp.bfloat16)
-        return jnp.concatenate([part, hot], axis=2).reshape(end - begin, lanes, WIDE)
-
-    decode_rows = jnp.pad(
-        decode_query.reshape(dec * heads, width), ((0, LANES - dec * heads), (0, WIDE - width))
-    )
-
-    held = lax.optimization_barrier((turn, *tables, *beside, *across))
-    turn, tables, held = held[0], held[1 : 1 + pages], held[1 + pages :]
+        some = slice(begin * groups, end * groups)
+        return jnp.concatenate([query[0, some], hot[some]], axis=2).reshape(end - begin, lanes, WIDE)
+
+    marked = mark(suffix_query, 0, steps - 1)
+    held = lax.optimization_barrier((turn, hot, marked, *tables, *beside, *across))
+    turn, hot, marked = held[:3]
+    tables, held = held[3 : 3 + pages], held[3 + pages :]
     beside, across = held[: pages - 1], held[pages - 1 :]
     far = stack(*across)
     ends = [send(far, hop) for hop in hops]
     own = [stack(message, *beside), far]
     other = [swap(array) for array in own]
-    early, far = lax.optimization_barrier((suffix_query, far))
-    marked = mark(early, 0, steps - 1)
-
-    def middle(marked, table, own, other, order, *state, loaded=()):
+
+    def middle(marked, decode_rows, table, own, other, order, *state, loaded=()):
         counts = [array.shape[0] for array in own]
         size = sum(counts) * block
+        decode_rows = hot if decode_rows is None else decode_rows
         inputs = [in_vmem(marked), in_vmem(decode_rows), table, *(loaded or (*own, *other)), *state]
         aliases = {len(inputs) - 2: 0, len(inputs) - 1: 1} if state else {}
         kept = () if loaded else ((size, WIDE), (lat, size))
@@ -421,22 +421,25 @@
         )(*inputs)
 
     orders = list(range(blocks - 2)), [blocks - 2, blocks - 1]
-    mixed, stat, *loaded = middle(marked, tables[0], own, other, orders[0])
-    later, stat = lax.optimization_barrier((suffix_query, stat))
+    mixed, stat, *loaded = middle(marked, None, tables[0], own, other, orders[0])
+    later, decode_rows, stat = lax.optimization_barrier((suffix_query, decode_query, stat))
     late = mark(later, steps - 1, steps)
+    decode_rows = jnp.pad(
+        decode_rows.reshape(dec * heads, width), ((0, LANES - dec * heads), (0, WIDE - width))
+    )
     mixed, stat, late, decode_rows, *ends = lax.optimization_barrier(
         (mixed, stat, late, decode_rows, *ends)
     )
     states = [
         (mixed, stat),
-        middle(late, tables[0], own, other, orders[1], loaded=loaded)[:2],
+        middle(late, decode_rows, tables[0], own, other, orders[1], loaded=loaded)[:2],
     ]
     own += ends
     other += [swap(array) for array in ends]
     for number in range(1, pages - 1):
         chosen = slice(1 + number, 2 + number)
         states = [
-            middle(part, tables[number], own[chosen], other[chosen], order, *state)[:2]
+            middle(part, decode_rows, tables[number], own[chosen], other[chosen], order, *state)[:2]
             for part, order, state in zip((marked, late), orders, states)
         ]
     counts = [array.shape[0] for array in own]

time: 24.2 us -> 25.8 us (1.066)
  waiting for transfers between devices: 0.52 us -> 3.28 us
  local copies, waits for them, and re-layouts: 2.19 us -> 1.61 us
  other arithmetic: 0.81 us -> 0.39 us
  starting transfers between devices: 8.61 us -> 8.35 us
    ppermute x5, waiting for transfers between devices: 0.51 us -> 2.7 us  [send(): lax.ppermute(array, 'context', [(rank, rank ^ hop) for rank in range(coun...]
    pad x1, local copies, waits for them, and re-layouts: 0.9 us -> 0.02 us  [on_device(): jnp.pad(decode_rows.reshape(dec * heads, width), ((0, LANES - dec * heads...]
    slice x4 -> x6, local copies, waits for them, and re-layouts: 0.98 us -> 1.59 us  [the longest x4 1.55 us: mark(): query[0, some]]
    ppermute x3, waiting for transfers between devices: 0.01 us -> 0.57 us  [swap(): return lax.ppermute(array, 'tensor', [(0, 1), (1, 0)])]
    convert_element_type x2 -> x0, other arithmetic: 0.41 us -> none  [mark(): (owner == lax.broadcasted_iota(jnp.int32, shape, 2)).astype(jnp.bfloat16)]
    iota x4 -> x0, local copies, waits for them, and re-layouts: 0.31 us -> none  [mark(): owner = lax.broadcasted_iota(jnp.int32, shape, 0) + begin * groups]
  transfers between devices with their start and end apart: 8 -> 8, of which waited for: 1 -> 2; matrix products, arithmetic and copies ran while one was open for 8% -> 2% of each run, Pallas kernels for 18% -> 17%
where the time goes in v2:
time: 25.8 us; the launch traced here: 25.6 us
  Pallas kernels  9.85 us (38%)
  starting transfers between devices  8.35 us (32%)
  waiting for transfers between devices  3.28 us (13%)
  between operations  2.07 us (8%)
  local copies, waits for them, and re-layouts  1.61 us (6%)
  other arithmetic  0.39 us (2%)
    ppermute x5, starting transfers between devices, send(): lax.ppermute(array, 'context', [(rank, rank ^ hop) for rank in range(coun...  7.72 us
    pallas_call x1, Pallas kernels, on_device(): pl.pallas_call(functools.partial(last_kernel, (counts, block, heads, dec,...  3.98 us
    pallas_call x2, Pallas kernels, middle(): pl.pallas_call(functools.partial(middle_kernel, (counts, block, WIDE - wi...  3.65 us
    ppermute x5, waiting for transfers between devices, send(): lax.ppermute(array, 'context', [(rank, rank ^ hop) for rank in range(coun...  2.7 us
    slice x4, local copies, waits for them, and re-layouts, mark(): query[0, some]  1.55 us
    pallas_call x1, Pallas kernels, on_device(): pl.pallas_call(pack_kernel, out_shape=pltpu.VMEM((rows, LANES), jnp.bfloa...  1.4 us
    pallas_call x1, Pallas kernels, on_device(): pl.pallas_call(functools.partial(table_kernel, (layout, tok, cached, bloc...  0.8 us
    ppermute x3, starting transfers between devices, swap(): return lax.ppermute(array, 'tensor', [(0, 1), (1, 0)])  0.63 us
  transfers between devices with their start and end apart: 8, of which 2 were waited for; matrix products, arithmetic and copies ran while one was open for 2% of the time, Pallas kernels for 17%

profile of v2, /device:TPU:0, one launch (start us, length us, event | category | flops | bytes accessed | tf_op | source)
XLA Modules:
  0.0 25.6 jit_solution(12829162663774242011)
XLA Ops:
  0.6 1.4 %shard_map.122.refs_0_ = bf16[208,128]{1,0:T(8,128)(2,1)S(1)} custom-call(bf16[448,576]{1,0:T(8,128)(2,1)} %down_ref.1, bf16[2,7168]{1,0:T(2,128)(2,1)} %bitcast.13, bf16[1,64,576]{2,1,0:T(8,128)(2,1)} %latent_ref.1, bf16[1,16,576]{2,1,0:T(8,128)(2,1)} %bitcast.14), custom_call_target="tpu_custom_call" | custom-call | tf_op jit(solution)/shard_map/pallas_call | solution.py:341
  2.0 5.1 %collective-permute-start.3 = (bf16[208,128]{1,0:T(8,128)(2,1)S(1)}, bf16[208,128]{1,0:T(8,128)(2,1)S(1)}, u32[]{:S(2)}, u32[]{:S(2)}) collective-permute-start(bf16[208,128]{1,0:T(8,128)(2,1)S(1)} %shard_map.122.refs_0_), channel_id=1, source_target_pairs={{0,12},{2,14},{4,8},{6,10},{8,4},{10,6},{12,0},{14,2},{1,13},{3,15... | collective-permute-start | bytes 159752 | tf_op jit(solution)/shard_map/ppermute | solution.py:350
  7.1 0.0 collective-permute-start.2
  7.1 0.6 %collective-permute-start.1 = (bf16[208,128]{1,0:T(8,128)(2,1)S(1)}, bf16[208,128]{1,0:T(8,128)(2,1)S(1)}, u32[]{:S(2)}, u32[]{:S(2)}) collective-permute-start(bf16[208,128]{1,0:T(8,128)(2,1)S(1)} %shard_map.122.refs_0_), channel_id=1, source_target_pairs={{0,4},{2,6},{4,0},{6,2},{8,12},{10,14},{12,8},{14,10},{1,5},{3,7},... | collective-permute-start | bytes 159752 | tf_op jit(solution)/shard_map/ppermute | solution.py:350
  7.7 1.7 %collective-permute-start = (bf16[208,128]{1,0:T(8,128)(2,1)S(1)}, bf16[208,128]{1,0:T(8,128)(2,1)S(1)}, u32[]{:S(2)}, u32[]{:S(2)}) collective-permute-start(bf16[208,128]{1,0:T(8,128)(2,1)S(1)} %shard_map.122.refs_0_), channel_id=1, source_target_pairs={{0,2},{2,0},{4,6},{6,4},{8,10},{10,8},{12,14},{14,12},{1,3},{3,1},... | collective-permute-start | bytes 159752 | tf_op jit(solution)/shard_map/ppermute | solution.py:350
  10.7 0.8 %shard_map.121 = (bf16[400,128]{1,0:T(8,128)(2,1)S(1)}, bf16[240,128]{1,0:T(8,128)(2,1)S(1)}, f32[2,2,64]{2,1,0:T(2,128)S(1)}, bf16[64,32,64]{2,1,0:T(8,128)(2,1)S(1)}) custom-call(s32[1,8]{1,0:T(1,128)} %hits_ref.1, s32[1]{0:T(128)S(6)} %copy.13.prefix_ref, s32[1]{0:T(128)S(6)} %copy.14.length_ref), custom_call_target="tpu_custom_call" | custom-call | tf_op jit(solution)/shard_map/pallas_call | solution.py:375
  11.5 0.0 slice-start
  11.5 1.5 %slice-done = bf16[1,48,32,576]{3,2,1,0:T(8,128)(2,1)S(1)} async-done(((bf16[1,64,32,576]{3,2,1,0:T(8,128)(2,1)}), bf16[1,48,32,576]{3,2,1,0:T(8,128)(2,1)S(1)}, s32[]{:S(2)}) %slice-start) | async-done | bytes 1769496 | tf_op jit(solution)/shard_map/slice | solution.py:389
  13.1 0.3 %pad_maximum_fusion.marked_ref = bf16[3,512,640]{2,1,0:T(8,128)(2,1)S(1)} fusion(bf16[3,512,64]{2,1,0:T(8,128)(2,1)S(1)} %bitcast.10, bf16[3,512,576]{2,1,0:T(8,128)(2,1)S(1)} %bitcast.8), kind=kLoop, calls=%fused_computation | loop fusion | flops 3932160 | bytes 3932160 | tf_op jit(solution)/shard_map/concatenate | solution.py:389
  13.4 0.0 collective-permute-done.3.refs_2_
  13.4 0.0 collective-permute-done.2.refs_1_
  13.4 0.0 collective-permute-done.1.refs_0_
  13.4 0.0 collective-permute-done.refs_1_
  13.4 0.1 collective-permute-start.5
  13.5 0.6 %collective-permute-start.4 = (bf16[2,208,128]{2,1,0:T(8,128)(2,1)S(1)}, bf16[2,208,128]{2,1,0:T(8,128)(2,1)S(1)}, u32[]{:S(2)}, u32[]{:S(2)}) collective-permute-start(bf16[2,208,128]{2,1,0:T(8,128)(2,1)S(1)} %shard_map.123.refs_0_), channel_id=1, source_target_pairs={{0,1},{1,0},{2,3},{3,2},{4,5},{5,4},{6,7},{7,6},{8,9},{9,8},{10,11... | collective-permute-start | bytes 319496 | tf_op jit(solution)/shard_map/ppermute | solution.py:353
  14.1 0.4 %collective-permute-start.6 = (bf16[3,208,128]{2,1,0:T(8,128)(2,1)S(1)}, bf16[3,208,128]{2,1,0:T(8,128)(2,1)S(1)}, u32[]{:S(2)}, u32[]{:S(2)}) collective-permute-start(bf16[3,208,128]{2,1,0:T(8,128)(2,1)S(1)} %shard_map.124.refs_1_), channel_id=1, source_target_pairs={{0,2},{2,0},{4,6},{6,4},{8,10},{10,8},{12,14},{14,12},{1,3},{3,1},... | collective-permute-start | bytes 479240 | tf_op jit(solution)/shard_map/ppermute | solution.py:350
  14.5 0.0 copy-start
  14.5 0.0 slice-start.1
  14.5 0.6 %collective-permute-done.4.refs_2_.refs_3_ = bf16[2,208,128]{2,1,0:T(8,128)(2,1)S(1)} collective-permute-done((bf16[2,208,128]{2,1,0:T(8,128)(2,1)S(1)}, bf16[2,208,128]{2,1,0:T(8,128)(2,1)S(1)}, u32[]{:S(2)}, u32[]{:S(2)}) %collective-permute-start.4) | collective-permute-done | bytes 106528 | tf_op jit(solution)/shard_map/ppermute | solution.py:353
  15.0 0.0 collective-permute-done.5.refs_3_.refs_4_
  15.0 2.3 %shard_map.125 = (f32[3,512,512]{2,1,0:T(8,128)S(1)}, f32[3,8,512]{2,1,0:T(8,128)S(1)}, bf16[400,640]{1,0:T(8,128)(2,1)S(1)}, bf16[512,400]{1,0:T(8,128)(2,1)S(1)}) custom-call(bf16[3,512,640]{2,1,0:T(8,128)(2,1)S(1)} %pad_maximum_fusion.marked_ref, bf16[64,32,64]{2,1,0:T(8,128)(2,1)S(1)} %get-tuple-element.35.decode_ref, ...), custom_call_target="tpu_custom_call" | custom-call | tf_op jit(solution)/shard_map/pallas_call | solution.py:408
  17.3 0.0 copy-done
  17.4 0.0 slice-done.1
  17.4 0.1 pad_maximum_fusion.1.marked_ref.late_ref
  17.5 2.7 %collective-permute-done.6.refs_2_ = bf16[3,208,128]{2,1,0:T(8,128)(2,1)S(1)} collective-permute-done((bf16[3,208,128]{2,1,0:T(8,128)(2,1)S(1)}, bf16[3,208,128]{2,1,0:T(8,128)(2,1)S(1)}, u32[]{:S(2)}, u32[]{:S(2)}) %collective-permute-start.6) | collective-permute-done | bytes 159776 | tf_op jit(solution)/shard_map/ppermute | solution.py:350
  20.2 0.0 collective-permute-start.7
  20.2 1.4 %shard_map.126 = (f32[2,512,512]{2,1,0:T(8,128)S(1)}, f32[2,8,512]{2,1,0:T(8,128)S(1)}) custom-call(bf16[1,512,640]{2,1,0:T(8,128)(2,1)S(1)} %pad_maximum_fusion.1.marked_ref.late_ref, bf16[128,640]{1,0:T(8,128)(2,1)S(1)} %pad.4.decode_ref, bf16[400,128]{1,0:T(8,128)(2,1)S(1)} %get-tuple-element.36.table_ref, ...), custom_call_target="tpu_custom_call" | custom-call | tf_op jit(solution)/shard_map/pallas_call | solution.py:408
  21.6 0.0 collective-permute-done.7.refs_5_
  21.6 4.0 %shard_map.127 = (bf16[1,64,32,512]{3,2,1,0:T(8,128)(2,1)}, bf16[1,2,32,512]{3,2,1,0:T(8,128)(2,1)}, bf16[1,2,576]{2,1,0:T(2,128)(2,1)}) custom-call(bf16[3,512,640]{2,1,0:T(8,128)(2,1)S(1)} %pad_maximum_fusion.marked_ref, bf16[1,512,640]{2,1,0:T(8,128)(2,1)S(1)} %pad_maximum_fusion.1.marked_ref.late_ref, bf16[128,640]{1,0:T(8,128)(2,1)S(1)} %pad.4.decode_ref, ...), custom_call_target="tpu_custom_call" | custom-call | tf_op jit(solution)/shard_map/pallas_call | solution.py:446
  (5 shorter events, 0.1 us)
Async XLA Ops:
  2.0 11.3 %collective-permute-start.3 = (bf16[208,128]{1,0:T(8,128)(2,1)S(1)}, bf16[208,128]{1,0:T(8,128)(2,1)S(1)}, u32[]{:S(2)}, u32[]{:S(2)}) collective-permute-start(bf16[208,128]{1,0:T(8,128)(2,1)S(1)} %shard_map.122.refs_0_), channel_id=1, source_target_pairs={{0,12},{2,14},{4,8},{6,10},{8,4},{10,6},{12,0},{14,2},{1,13},{3,15... | collective-permute-start | bytes 159752 | tf_op jit(solution)/shard_map/ppermute | solution.py:350
  7.1 6.3 %collective-permute-start.2 = (bf16[208,128]{1,0:T(8,128)(2,1)S(1)}, bf16[208,128]{1,0:T(8,128)(2,1)S(1)}, u32[]{:S(2)}, u32[]{:S(2)}) collective-permute-start(bf16[208,128]{1,0:T(8,128)(2,1)S(1)} %shard_map.122.refs_0_), channel_id=1, source_target_pairs={{0,8},{2,10},{4,12},{6,14},{8,0},{10,2},{12,4},{14,6},{1,9},{3,11}... | collective-permute-start | bytes 159752 | tf_op jit(solution)/shard_map/ppermute | solution.py:350
  7.1 6.3 %collective-permute-start.1 = (bf16[208,128]{1,0:T(8,128)(2,1)S(1)}, bf16[208,128]{1,0:T(8,128)(2,1)S(1)}, u32[]{:S(2)}, u32[]{:S(2)}) collective-permute-start(bf16[208,128]{1,0:T(8,128)(2,1)S(1)} %shard_map.122.refs_0_), channel_id=1, source_target_pairs={{0,4},{2,6},{4,0},{6,2},{8,12},{10,14},{12,8},{14,10},{1,5},{3,7},... | collective-permute-start | bytes 159752 | tf_op jit(solution)/shard_map/ppermute | solution.py:350
  7.7 5.7 %collective-permute-start = (bf16[208,128]{1,0:T(8,128)(2,1)S(1)}, bf16[208,128]{1,0:T(8,128)(2,1)S(1)}, u32[]{:S(2)}, u32[]{:S(2)}) collective-permute-start(bf16[208,128]{1,0:T(8,128)(2,1)S(1)} %shard_map.122.refs_0_), channel_id=1, source_target_pairs={{0,2},{2,0},{4,6},{6,4},{8,10},{10,8},{12,14},{14,12},{1,3},{3,1},... | collective-permute-start | bytes 159752 | tf_op jit(solution)/shard_map/ppermute | solution.py:350
  11.5 1.5 %slice-start = ((bf16[1,64,32,576]{3,2,1,0:T(8,128)(2,1)}), bf16[1,48,32,576]{3,2,1,0:T(8,128)(2,1)S(1)}, s32[]{:S(2)}) async-start(bf16[1,64,32,576]{3,2,1,0:T(8,128)(2,1)} %param.15), calls=%async_computation | async-start | bytes 3932160 | tf_op jit(solution)/shard_map/slice | solution.py:389
  13.4 1.6 %collective-permute-start.5 = (bf16[3,208,128]{2,1,0:T(8,128)(2,1)S(1)}, bf16[3,208,128]{2,1,0:T(8,128)(2,1)S(1)}, u32[]{:S(2)}, u32[]{:S(2)}) collective-permute-start(bf16[3,208,128]{2,1,0:T(8,128)(2,1)S(1)} %shard_map.124.refs_1_), channel_id=1, source_target_pairs={{0,1},{1,0},{2,3},{3,2},{4,5},{5,4},{6,7},{7,6},{8,9},{9,8},{10,11... | collective-permute-start | bytes 479240 | tf_op jit(solution)/shard_map/ppermute | solution.py:353
  13.5 1.5 %collective-permute-start.4 = (bf16[2,208,128]{2,1,0:T(8,128)(2,1)S(1)}, bf16[2,208,128]{2,1,0:T(8,128)(2,1)S(1)}, u32[]{:S(2)}, u32[]{:S(2)}) collective-permute-start(bf16[2,208,128]{2,1,0:T(8,128)(2,1)S(1)} %shard_map.123.refs_0_), channel_id=1, source_target_pairs={{0,1},{1,0},{2,3},{3,2},{4,5},{5,4},{6,7},{7,6},{8,9},{9,8},{10,11... | collective-permute-start | bytes 319496 | tf_op jit(solution)/shard_map/ppermute | solution.py:353
  14.1 6.1 %collective-permute-start.6 = (bf16[3,208,128]{2,1,0:T(8,128)(2,1)S(1)}, bf16[3,208,128]{2,1,0:T(8,128)(2,1)S(1)}, u32[]{:S(2)}, u32[]{:S(2)}) collective-permute-start(bf16[3,208,128]{2,1,0:T(8,128)(2,1)S(1)} %shard_map.124.refs_1_), channel_id=1, source_target_pairs={{0,2},{2,0},{4,6},{6,4},{8,10},{10,8},{12,14},{14,12},{1,3},{3,1},... | collective-permute-start | bytes 479240 | tf_op jit(solution)/shard_map/ppermute | solution.py:350
  14.5 2.9 %copy-start = (bf16[1,2,32,576]{3,2,1,0:T(8,128)(2,1)S(1)}, bf16[1,2,32,576]{3,2,1,0:T(8,128)(2,1)}, u32[]{:S(2)}) copy-start(bf16[1,2,32,576]{3,2,1,0:T(8,128)(2,1)} %param.19) | copy-start | bytes 221188
  14.5 2.9 %slice-start.1 = ((bf16[1,64,32,576]{3,2,1,0:T(8,128)(2,1)}), bf16[1,16,32,576]{3,2,1,0:T(8,128)(2,1)S(1)}, s32[]{:S(2)}) async-start(bf16[1,64,32,576]{3,2,1,0:T(8,128)(2,1)} %param.15), calls=%async_computation.1 | async-start | bytes 1310720 | tf_op jit(solution)/shard_map/slice | solution.py:389
  20.2 1.4 %collective-permute-start.7 = (bf16[3,208,128]{2,1,0:T(8,128)(2,1)S(1)}, bf16[3,208,128]{2,1,0:T(8,128)(2,1)S(1)}, u32[]{:S(2)}, u32[]{:S(2)}) collective-permute-start(bf16[3,208,128]{2,1,0:T(8,128)(2,1)S(1)} %collective-permute-done.6.refs_2_), channel_id=1, source_target_pairs={{0,1},{1,0},{2,3},{3,2},{4,5},{5,4},{6,7},{7,6},{8,9},{9,8},{10,11... | collective-permute-start | bytes 479240 | tf_op jit(solution)/shard_map/ppermute | solution.py:353

commit v3 on v2

--- a/solution.py
+++ b/solution.py
@@ -115,12 +115,26 @@
     mixed_ref[block, :, :lanes] = state[2]
 
 
-def table_kernel(shape, hits_ref, prefix_ref, length_ref, *refs):
+def table_kernel(shape, prefix_ref, length_ref, hits_hbm, gain_hbm, query_hbm, *refs):
     layout, tok, cached, block_rows = shape
-    *table_refs, turn_ref, hot_ref = refs
+    *table_refs, turn_ref, hot_ref, marked_ref, gain_ref, query_ref, hits_ref, sem, side_sem = refs
+    steps, groups, heads, width = query_ref.shape
+
+    def fetch(step):
+        return pltpu.make_async_copy(
+            query_hbm.at[0, pl.ds(step * groups, groups)], query_ref.at[step], sem.at[step]
+        )
+
+    fetch_hits = pltpu.make_async_copy(hits_hbm, hits_ref, side_sem.at[0])
+    fetch_gain = pltpu.make_async_copy(gain_hbm, gain_ref, side_sem.at[1])
+    fetch_hits.start()
+    for step in range(steps):
+        fetch(step).start()
+    fetch_gain.start()
     token = lax.broadcasted_iota(jnp.int32, hot_ref.shape, 0)
     hot = token == lax.broadcasted_iota(jnp.int32, hot_ref.shape, 2)
     hot_ref[...] = jnp.where(hot, 1.0, 0.0).astype(jnp.bfloat16)
+    fetch_hits.wait()
     me = lax.axis_index("context")
     prefix = prefix_ref[0]
     length = length_ref[0]
@@ -156,10 +170,22 @@
     sine = jnp.sin(angle)
     turn_ref[1] = jnp.where(lane < half, -sine, sine)
 
+    rows = groups * heads
+    for step in range(steps):
+        fetch(step).wait()
+        mark = hot_ref[step * groups : (step + 1) * groups].reshape(rows, WIDE - width)
+        marked_ref[step] = jnp.concatenate([query_ref[step].reshape(rows, width), mark], axis=1)
+    fetch_gain.wait()
+
 
 def swap_halves(x):
     half = x.shape[1] // 2
     return jnp.concatenate([x[:, half:], x[:, :half]], axis=1)
+
+
+def pick_block(marked_ref, late_ref, block):
+    count = marked_ref.shape[0]
+    return marked_ref[block] if block < count else late_ref[block - count]
 
 
 def load_keys(keys_ref, pairs, table_ref, rows, side):
@@ -182,7 +208,7 @@
         at += rows
 
 
-def middle_kernel(shape, marked_ref, decode_ref, table_ref, *refs):
+def middle_kernel(shape, marked_ref, late_ref, decode_ref, table_ref, *refs):
     counts, rows, side, order, blocks, loaded = shape
     kinds = len(counts)
     if loaded:
@@ -206,7 +232,7 @@
     def begin(index):
         if order[index] == blocks - 1:
             return score(keys, decode_ref[...]) + table_ref[...].astype(jnp.float32)
-        return score(keys, marked_ref[index])
+        return score(keys, pick_block(marked_ref, late_ref, order[index]))
 
     def finish(index, scores):
         lanes = lanes_of(index)
@@ -276,7 +302,7 @@
     def begin(block):
         if block == steps:
             return score(keys_ref[...], decode_ref[...]) + table_ref[...].astype(jnp.float32)
-        return score(keys_ref[...], marked_ref[block] if block < cut else late_ref[block - cut])
+        return score(keys_ref[...], pick_block(marked_ref, late_ref, block))
 
     def finish(block, scores):
         half, index = (0, block) if block < cut else (1, block - cut)
@@ -352,13 +378,14 @@
     def swap(array):
         return lax.ppermute(array, "tensor", [(0, 1), (1, 0)])
 
-    def stack(*arrays):
+    def stack(*arrays, cost=None):
         return pl.pallas_call(
             stack_kernel,
             out_shape=pltpu.VMEM((len(arrays), rows, LANES), jnp.bfloat16),
             in_specs=[vmem] * len(arrays),
             out_specs=vmem,
             compiler_params=small,
+            cost_estimate=cost,
         )(*arrays)
 
     hops = list(range(1, pages))
@@ -372,37 +399,55 @@
     lanes = groups * heads
     blocks = steps + 1
 
-    *tables, turn, hot = pl.pallas_call(
+    first_steps = steps // 2
+    *tables, turn, hot, marked, gain = pl.pallas_call(
         functools.partial(table_kernel, (layout, tok, cached, block_rows)),
         out_shape=tuple(pltpu.VMEM((len(keys) * block, LANES), jnp.bfloat16) for keys in layout)
         + (
             pltpu.VMEM((2, dec, width - lat), jnp.float32),
             pltpu.VMEM((tok, heads, WIDE - width), jnp.bfloat16),
+            pltpu.VMEM((first_steps, lanes, WIDE), jnp.bfloat16),
+            pltpu.VMEM((1, lat), jnp.float32),
         ),
-        in_specs=[smem, smem, smem],
-        out_specs=(vmem,) * (len(layout) + 2),
-        compiler_params=small,
-    )(in_hbm(hit_slots), prefix_blocks, suffix_len)
+        in_specs=[smem, smem, anywhere, anywhere, anywhere],
+        out_specs=(vmem,) * (len(layout) + 4),
+        scratch_shapes=[
+            pltpu.VMEM((first_steps, groups, heads, width), jnp.bfloat16),
+            pltpu.SMEM(hit_slots.shape, jnp.int32),
+            pltpu.SemaphoreType.DMA((first_steps,)),
+            pltpu.SemaphoreType.DMA((2,)),
+        ],
+        compiler_params=large,
+    )(
+        prefix_blocks,
+        suffix_len,
+        in_hbm(hit_slots),
+        in_hbm(kv_gain.reshape(1, lat)),
+        in_hbm(suffix_query),
+    )
 
     def mark(query, begin, end):
         some = slice(begin * groups, end * groups)
         return jnp.concatenate([query[0, some], hot[some]], axis=2).reshape(end - begin, lanes, WIDE)
 
-    marked = mark(suffix_query, 0, steps - 1)
     held = lax.optimization_barrier((turn, hot, marked, *tables, *beside, *across))
     turn, hot, marked = held[:3]
     tables, held = held[3 : 3 + pages], held[3 + pages :]
     beside, across = held[: pages - 1], held[pages - 1 :]
     far = stack(*across)
     ends = [send(far, hop) for hop in hops]
-    own = [stack(message, *beside), far]
+    cost = pl.CostEstimate(flops=6 * 10**8, bytes_accessed=1 << 20, transcendentals=0)
+    own = [stack(message, *beside, cost=cost), far]
     other = [swap(array) for array in own]
-
-    def middle(marked, decode_rows, table, own, other, order, *state, loaded=()):
+    later, far = lax.optimization_barrier((suffix_query, far))
+    late = mark(later, first_steps, steps)
+
+    def middle(decode_rows, table, own, other, order, *state, loaded=()):
         counts = [array.shape[0] for array in own]
         size = sum(counts) * block
         decode_rows = hot if decode_rows is None else decode_rows
-        inputs = [in_vmem(marked), in_vmem(decode_rows), table, *(loaded or (*own, *other)), *state]
+        inputs = [in_vmem(marked), in_vmem(late), in_vmem(decode_rows), table]
+        inputs += [*(loaded or (*own, *other)), *state]
         aliases = {len(inputs) - 2: 0, len(inputs) - 1: 1} if state else {}
         kept = () if loaded else ((size, WIDE), (lat, size))
         return pl.pallas_call(
@@ -421,26 +466,23 @@
         )(*inputs)
 
     orders = list(range(blocks - 2)), [blocks - 2, blocks - 1]
-    mixed, stat, *loaded = middle(marked, None, tables[0], own, other, orders[0])
-    later, decode_rows, stat = lax.optimization_barrier((suffix_query, decode_query, stat))
-    late = mark(later, steps - 1, steps)
+    mixed, stat, *loaded = middle(None, tables[0], own, other, orders[0])
+    decode_rows, stat = lax.optimization_barrier((decode_query, stat))
     decode_rows = jnp.pad(
         decode_rows.reshape(dec * heads, width), ((0, LANES - dec * heads), (0, WIDE - width))
     )
-    mixed, stat, late, decode_rows, *ends = lax.optimization_barrier(
-        (mixed, stat, late, decode_rows, *ends)
-    )
+    mixed, stat, decode_rows, *ends = lax.optimization_barrier((mixed, stat, decode_rows, *ends))
     states = [
         (mixed, stat),
-        middle(late, decode_rows, tables[0], own, other, orders[1], loaded=loaded)[:2],
+        middle(decode_rows, tables[0], own, other, orders[1], loaded=loaded)[:2],
     ]
     own += ends
     other += [swap(array) for array in ends]
     for number in range(1, pages - 1):
         chosen = slice(1 + number, 2 + number)
         states = [
-            middle(part, decode_rows, tables[number], own[chosen], other[chosen], order, *state)[:2]
-            for part, order, state in zip((marked, late), orders, states)
+            middle(decode_rows, tables[number], own[chosen], other[chosen], order, *state)[:2]
+            for order, state in zip(orders, states)
         ]
     counts = [array.shape[0] for array in own]
     return pl.pallas_call(
@@ -460,7 +502,7 @@
             pltpu.SemaphoreType.DMA((blocks, 2)),
         ],
         compiler_params=large,
-    )(in_vmem(marked), in_vmem(late), in_vmem(decode_rows), tables[-1], turn, in_hbm(kv_gain.reshape(1, lat)), *own, *other, *states[0], *states[1])
+    )(in_vmem(marked), in_vmem(late), in_vmem(decode_rows), tables[-1], turn, gain, *own, *other, *states[0], *states[1])
 
 
 def solution(mesh):

time: 25.8 us -> 23.2 us (0.90)
  waiting for transfers between devices: 3.28 us -> 0.04 us
  starting transfers between devices: 8.35 us -> 10 us
  local copies, waits for them, and re-layouts: 1.61 us -> 0.76 us
    ppermute x5, waiting for transfers between devices: 2.7 us -> 0.01 us  [send(): lax.ppermute(array, 'context', [(rank, rank ^ hop) for rank in range(coun...]
    ppermute x5, starting transfers between devices: 7.72 us -> 8.87 us  [send(): lax.ppermute(array, 'context', [(rank, rank ^ hop) for rank in range(coun...]
    slice x4 -> x2, local copies, waits for them, and re-layouts: 1.55 us -> 0.72 us  [mark(): query[0, some]]
    pallas_call x1, Pallas kernels: 0.8 us -> 1.46 us  [on_device(): pl.pallas_call(functools.partial(table_kernel, (layout, tok, cached, bloc...]
    pallas_call x1, Pallas kernels: 3.98 us -> 3.36 us  [on_device(): pl.pallas_call(functools.partial(last_kernel, (counts, block, heads, dec,...]
    ppermute x3, waiting for transfers between devices: 0.57 us -> 0.03 us  [swap(): return lax.ppermute(array, 'tensor', [(0, 1), (1, 0)])]
    ppermute x3, starting transfers between devices: 0.63 us -> 1.14 us  [swap(): return lax.ppermute(array, 'tensor', [(0, 1), (1, 0)])]
  transfers between devices with their start and end apart: 8 -> 8, of which waited for: 2 -> 0; matrix products, arithmetic and copies ran while one was open for 2% -> 1% of each run, Pallas kernels for 17% -> 22%
where the time goes in v3:
time: 23.2 us; the launch traced here: 22.9 us
  starting transfers between devices  10 us (43%)
  Pallas kernels  9.89 us (43%)
  between operations  2.05 us (9%)
  local copies, waits for them, and re-layouts  0.76 us (3%)
    ppermute x5, starting transfers between devices, send(): lax.ppermute(array, 'context', [(rank, rank ^ hop) for rank in range(coun...  8.87 us
    pallas_call x2, Pallas kernels, middle(): pl.pallas_call(functools.partial(middle_kernel, (counts, block, WIDE - wi...  3.65 us
    pallas_call x1, Pallas kernels, on_device(): pl.pallas_call(functools.partial(last_kernel, (counts, block, heads, dec,...  3.36 us
    pallas_call x1, Pallas kernels, on_device(): pl.pallas_call(functools.partial(table_kernel, (layout, tok, cached, bloc...  1.46 us
    pallas_call x1, Pallas kernels, on_device(): pl.pallas_call(pack_kernel, out_shape=pltpu.VMEM((rows, LANES), jnp.bfloa...  1.4 us
    ppermute x3, starting transfers between devices, swap(): return lax.ppermute(array, 'tensor', [(0, 1), (1, 0)])  1.14 us
    slice x2, local copies, waits for them, and re-layouts, mark(): query[0, some]  0.72 us
  transfers between devices with their start and end apart: 8, of which 0 were waited for; matrix products, arithmetic and copies ran while one was open for 1% of the time, Pallas kernels for 22%

profile of v3, /device:TPU:0, one launch (start us, length us, event | category | flops | bytes accessed | tf_op | source)
XLA Modules:
  0.0 22.9 jit_solution(17028166480325906041)
XLA Ops:
  0.6 1.4 %shard_map.122.refs_0_ = bf16[208,128]{1,0:T(8,128)(2,1)S(1)} custom-call(bf16[448,576]{1,0:T(8,128)(2,1)} %down_ref.1, bf16[2,7168]{1,0:T(2,128)(2,1)} %bitcast.9, bf16[1,64,576]{2,1,0:T(8,128)(2,1)} %latent_ref.1, bf16[1,16,576]{2,1,0:T(8,128)(2,1)} %bitcast.10), custom_call_target="tpu_custom_call" | custom-call | tf_op jit(solution)/shard_map/pallas_call | solution.py:367
  2.0 5.1 %collective-permute-start.3 = (bf16[208,128]{1,0:T(8,128)(2,1)S(1)}, bf16[208,128]{1,0:T(8,128)(2,1)S(1)}, u32[]{:S(2)}, u32[]{:S(2)}) collective-permute-start(bf16[208,128]{1,0:T(8,128)(2,1)S(1)} %shard_map.122.refs_0_), channel_id=1, source_target_pairs={{0,12},{2,14},{4,8},{6,10},{8,4},{10,6},{12,0},{14,2},{1,13},{3,15... | collective-permute-start | bytes 159752 | tf_op jit(solution)/shard_map/ppermute | solution.py:376
  7.1 0.0 collective-permute-start.2
  7.1 0.6 %collective-permute-start.1 = (bf16[208,128]{1,0:T(8,128)(2,1)S(1)}, bf16[208,128]{1,0:T(8,128)(2,1)S(1)}, u32[]{:S(2)}, u32[]{:S(2)}) collective-permute-start(bf16[208,128]{1,0:T(8,128)(2,1)S(1)} %shard_map.122.refs_0_), channel_id=1, source_target_pairs={{0,4},{2,6},{4,0},{6,2},{8,12},{10,14},{12,8},{14,10},{1,5},{3,7},... | collective-permute-start | bytes 159752 | tf_op jit(solution)/shard_map/ppermute | solution.py:376
  7.7 1.7 %collective-permute-start = (bf16[208,128]{1,0:T(8,128)(2,1)S(1)}, bf16[208,128]{1,0:T(8,128)(2,1)S(1)}, u32[]{:S(2)}, u32[]{:S(2)}) collective-permute-start(bf16[208,128]{1,0:T(8,128)(2,1)S(1)} %shard_map.122.refs_0_), channel_id=1, source_target_pairs={{0,2},{2,0},{4,6},{6,4},{8,10},{10,8},{12,14},{14,12},{1,3},{3,1},... | collective-permute-start | bytes 159752 | tf_op jit(solution)/shard_map/ppermute | solution.py:376
  10.7 1.5 %shard_map.121 = (bf16[400,128]{1,0:T(8,128)(2,1)S(1)}, bf16[240,128]{1,0:T(8,128)(2,1)S(1)}, f32[2,2,64]{2,1,0:T(2,128)S(1)}, bf16[64,32,64]{2,1,0:T(8,128)(2,1...) custom-call(s32[1]{0:T(128)S(6)} %copy.13.prefix_ref, s32[1]{0:T(128)S(6)} %copy.14.length_ref, ...), custom_call_target="tpu_custom_call" | custom-call | tf_op jit(solution)/shard_map/pallas_call | solution.py:403
  12.2 0.0 collective-permute-done.3.refs_2_
  12.2 0.0 collective-permute-done.2.refs_1_
  12.2 0.0 collective-permute-done.1.refs_0_
  12.2 0.0 collective-permute-done.refs_1_
  12.2 1.5 %collective-permute-start.6 = (bf16[3,208,128]{2,1,0:T(8,128)(2,1)S(1)}, bf16[3,208,128]{2,1,0:T(8,128)(2,1)S(1)}, u32[]{:S(2)}, u32[]{:S(2)}) collective-permute-start(bf16[3,208,128]{2,1,0:T(8,128)(2,1)S(1)} %shard_map.123.refs_1_), channel_id=1, source_target_pairs={{0,2},{2,0},{4,6},{6,4},{8,10},{10,8},{12,14},{14,12},{1,3},{3,1},... | collective-permute-start | bytes 479240 | tf_op jit(solution)/shard_map/ppermute | solution.py:376
  13.7 0.0 collective-permute-start.5
  13.7 0.0 slice-start
  13.8 0.6 %collective-permute-start.4 = (bf16[2,208,128]{2,1,0:T(8,128)(2,1)S(1)}, bf16[2,208,128]{2,1,0:T(8,128)(2,1)S(1)}, u32[]{:S(2)}, u32[]{:S(2)}) collective-permute-start(bf16[2,208,128]{2,1,0:T(8,128)(2,1)S(1)} %shard_map.124.refs_0_), channel_id=1, source_target_pairs={{0,1},{1,0},{2,3},{3,2},{4,5},{5,4},{6,7},{7,6},{8,9},{9,8},{10,11... | collective-permute-start | bytes 319496 | tf_op jit(solution)/shard_map/ppermute | solution.py:379
  14.4 0.7 %slice-done = bf16[1,32,32,576]{3,2,1,0:T(8,128)(2,1)S(1)} async-done(((bf16[1,64,32,576]{3,2,1,0:T(8,128)(2,1)}), bf16[1,32,32,576]{3,2,1,0:T(8,128)(2,1)S(1)}, s32[]{:S(2)}) %slice-start) | async-done | bytes 1179672 | tf_op jit(solution)/shard_map/slice | solution.py:431
  15.1 0.2 pad_maximum_fusion.late_ref
  15.3 0.0 copy-start
  15.3 0.0 collective-permute-done.4.refs_2_.refs_3_
  15.3 0.0 collective-permute-done.5.refs_3_.refs_4_
  15.3 2.3 %shard_map.125 = (f32[3,512,512]{2,1,0:T(8,128)S(1)}, f32[3,8,512]{2,1,0:T(8,128)S(1)}, bf16[400,640]{1,0:T(8,128)(2,1)S(1)}, bf16[512,400]{1,0:T(8,128)(2,1)S(1)}) custom-call(bf16[2,512,640]{2,1,0:T(8,128)(2,1)S(1)} %get-tuple-element.36.marked_ref, bf16[2,512,640]{2,1,0:T(8,128)(2,1)S(1)} %pad_maximum_fusion.late_ref, ...), custom_call_target="tpu_custom_call" | custom-call | tf_op jit(solution)/shard_map/pallas_call | solution.py:453
  17.6 0.0 copy-done
  17.6 0.0 collective-permute-done.6.refs_2_
  17.6 0.6 %collective-permute-start.7 = (bf16[3,208,128]{2,1,0:T(8,128)(2,1)S(1)}, bf16[3,208,128]{2,1,0:T(8,128)(2,1)S(1)}, u32[]{:S(2)}, u32[]{:S(2)}) collective-permute-start(bf16[3,208,128]{2,1,0:T(8,128)(2,1)S(1)} %collective-permute-done.6.refs_2_), channel_id=1, source_target_pairs={{0,1},{1,0},{2,3},{3,2},{4,5},{5,4},{6,7},{7,6},{8,9},{9,8},{10,11... | collective-permute-start | bytes 479240 | tf_op jit(solution)/shard_map/ppermute | solution.py:379
  18.2 1.4 %shard_map.126 = (f32[2,512,512]{2,1,0:T(8,128)S(1)}, f32[2,8,512]{2,1,0:T(8,128)S(1)}) custom-call(bf16[2,512,640]{2,1,0:T(8,128)(2,1)S(1)} %get-tuple-element.36.marked_ref, bf16[2,512,640]{2,1,0:T(8,128)(2,1)S(1)} %pad_maximum_fusion.late_ref, bf16[128,640]{1,0:T(8,128)(2,1)S(1)} %pad.4.decode_ref, bf16[400,128]{1,0:T(8,128)(2,1)S(1)} %get-tuple-element.42.table_ref, ...), custom_call_target="tpu_custom_call" | custom-call | tf_op jit(solution)/shard_map/pallas_call | solution.py:453
  19.6 0.0 collective-permute-done.7.refs_5_
  19.6 3.4 %shard_map.127 = (bf16[1,64,32,512]{3,2,1,0:T(8,128)(2,1)}, bf16[1,2,32,512]{3,2,1,0:T(8,128)(2,1)}, bf16[1,2,576]{2,1,0:T(2,128)(2,1)}) custom-call(bf16[2,512,640]{2,1,0:T(8,128)(2,1)S(1)} %get-tuple-element.36.marked_ref, bf16[2,512,640]{2,1,0:T(8,128)(2,1)S(1)} %pad_maximum_fusion.late_ref, bf16[128,640]{1,0:T(8,128)(2,1)S(1)} %pad.4.decode_ref, ...), custom_call_target="tpu_custom_call" | custom-call | tf_op jit(solution)/shard_map/pallas_call | solution.py:488
  (4 shorter events, 0.1 us)
Async XLA Ops:
  2.0 10.1 %collective-permute-start.3 = (bf16[208,128]{1,0:T(8,128)(2,1)S(1)}, bf16[208,128]{1,0:T(8,128)(2,1)S(1)}, u32[]{:S(2)}, u32[]{:S(2)}) collective-permute-start(bf16[208,128]{1,0:T(8,128)(2,1)S(1)} %shard_map.122.refs_0_), channel_id=1, source_target_pairs={{0,12},{2,14},{4,8},{6,10},{8,4},{10,6},{12,0},{14,2},{1,13},{3,15... | collective-permute-start | bytes 159752 | tf_op jit(solution)/shard_map/ppermute | solution.py:376
  7.1 5.1 %collective-permute-start.2 = (bf16[208,128]{1,0:T(8,128)(2,1)S(1)}, bf16[208,128]{1,0:T(8,128)(2,1)S(1)}, u32[]{:S(2)}, u32[]{:S(2)}) collective-permute-start(bf16[208,128]{1,0:T(8,128)(2,1)S(1)} %shard_map.122.refs_0_), channel_id=1, source_target_pairs={{0,8},{2,10},{4,12},{6,14},{8,0},{10,2},{12,4},{14,6},{1,9},{3,11}... | collective-permute-start | bytes 159752 | tf_op jit(solution)/shard_map/ppermute | solution.py:376
  7.1 5.1 %collective-permute-start.1 = (bf16[208,128]{1,0:T(8,128)(2,1)S(1)}, bf16[208,128]{1,0:T(8,128)(2,1)S(1)}, u32[]{:S(2)}, u32[]{:S(2)}) collective-permute-start(bf16[208,128]{1,0:T(8,128)(2,1)S(1)} %shard_map.122.refs_0_), channel_id=1, source_target_pairs={{0,4},{2,6},{4,0},{6,2},{8,12},{10,14},{12,8},{14,10},{1,5},{3,7},... | collective-permute-start | bytes 159752 | tf_op jit(solution)/shard_map/ppermute | solution.py:376
  7.7 4.5 %collective-permute-start = (bf16[208,128]{1,0:T(8,128)(2,1)S(1)}, bf16[208,128]{1,0:T(8,128)(2,1)S(1)}, u32[]{:S(2)}, u32[]{:S(2)}) collective-permute-start(bf16[208,128]{1,0:T(8,128)(2,1)S(1)} %shard_map.122.refs_0_), channel_id=1, source_target_pairs={{0,2},{2,0},{4,6},{6,4},{8,10},{10,8},{12,14},{14,12},{1,3},{3,1},... | collective-permute-start | bytes 159752 | tf_op jit(solution)/shard_map/ppermute | solution.py:376
  12.2 5.4 %collective-permute-start.6 = (bf16[3,208,128]{2,1,0:T(8,128)(2,1)S(1)}, bf16[3,208,128]{2,1,0:T(8,128)(2,1)S(1)}, u32[]{:S(2)}, u32[]{:S(2)}) collective-permute-start(bf16[3,208,128]{2,1,0:T(8,128)(2,1)S(1)} %shard_map.123.refs_1_), channel_id=1, source_target_pairs={{0,2},{2,0},{4,6},{6,4},{8,10},{10,8},{12,14},{14,12},{1,3},{3,1},... | collective-permute-start | bytes 479240 | tf_op jit(solution)/shard_map/ppermute | solution.py:376
  13.7 1.6 %collective-permute-start.5 = (bf16[3,208,128]{2,1,0:T(8,128)(2,1)S(1)}, bf16[3,208,128]{2,1,0:T(8,128)(2,1)S(1)}, u32[]{:S(2)}, u32[]{:S(2)}) collective-permute-start(bf16[3,208,128]{2,1,0:T(8,128)(2,1)S(1)} %shard_map.123.refs_1_), channel_id=1, source_target_pairs={{0,1},{1,0},{2,3},{3,2},{4,5},{5,4},{6,7},{7,6},{8,9},{9,8},{10,11... | collective-permute-start | bytes 479240 | tf_op jit(solution)/shard_map/ppermute | solution.py:379
  13.7 1.3 %slice-start = ((bf16[1,64,32,576]{3,2,1,0:T(8,128)(2,1)}), bf16[1,32,32,576]{3,2,1,0:T(8,128)(2,1)S(1)}, s32[]{:S(2)}) async-start(bf16[1,64,32,576]{3,2,1,0:T(8,128)(2,1)} %query_hbm.1), calls=%async_computation | async-start | bytes 2621440 | tf_op jit(solution)/shard_map/slice | solution.py:431
  13.8 1.5 %collective-permute-start.4 = (bf16[2,208,128]{2,1,0:T(8,128)(2,1)S(1)}, bf16[2,208,128]{2,1,0:T(8,128)(2,1)S(1)}, u32[]{:S(2)}, u32[]{:S(2)}) collective-permute-start(bf16[2,208,128]{2,1,0:T(8,128)(2,1)S(1)} %shard_map.124.refs_0_), channel_id=1, source_target_pairs={{0,1},{1,0},{2,3},{3,2},{4,5},{5,4},{6,7},{7,6},{8,9},{9,8},{10,11... | collective-permute-start | bytes 319496 | tf_op jit(solution)/shard_map/ppermute | solution.py:379
  15.3 2.3 %copy-start = (bf16[1,2,32,576]{3,2,1,0:T(8,128)(2,1)S(1)}, bf16[1,2,32,576]{3,2,1,0:T(8,128)(2,1)}, u32[]{:S(2)}) copy-start(bf16[1,2,32,576]{3,2,1,0:T(8,128)(2,1)} %param.19) | copy-start | bytes 221188
  17.6 1.9 %collective-permute-start.7 = (bf16[3,208,128]{2,1,0:T(8,128)(2,1)S(1)}, bf16[3,208,128]{2,1,0:T(8,128)(2,1)S(1)}, u32[]{:S(2)}, u32[]{:S(2)}) collective-permute-start(bf16[3,208,128]{2,1,0:T(8,128)(2,1)S(1)} %collective-permute-done.6.refs_2_), channel_id=1, source_target_pairs={{0,1},{1,0},{2,3},{3,2},{4,5},{5,4},{6,7},{7,6},{8,9},{9,8},{10,11... | collective-permute-start | bytes 479240 | tf_op jit(solution)/shard_map/ppermute | solution.py:379

commit v4 on v3

--- a/solution.py
+++ b/solution.py
@@ -399,7 +399,7 @@
     lanes = groups * heads
     blocks = steps + 1
 
-    first_steps = steps // 2
+    first_steps = steps - 1
     *tables, turn, hot, marked, gain = pl.pallas_call(
         functools.partial(table_kernel, (layout, tok, cached, block_rows)),
         out_shape=tuple(pltpu.VMEM((len(keys) * block, LANES), jnp.bfloat16) for keys in layout)

time: 23.2 us -> 23 us (level)
  waiting for transfers between devices: 0.04 us -> 1.01 us
  local copies, waits for them, and re-layouts: 0.76 us -> 0.04 us
  starting transfers between devices: 10 us -> 9.47 us
    ppermute x3, waiting for transfers between devices: 0.03 us -> 0.81 us  [swap(): return lax.ppermute(array, 'tensor', [(0, 1), (1, 0)])]
    slice x2, local copies, waits for them, and re-layouts: 0.72 us -> 0.01 us  [mark(): query[0, some]]
    ppermute x3, starting transfers between devices: 1.14 us -> 0.82 us  [swap(): return lax.ppermute(array, 'tensor', [(0, 1), (1, 0)])]
  transfers between devices with their start and end apart: 8 -> 8, of which waited for: 0 -> 2; matrix products, arithmetic and copies ran while one was open for 1% -> 1% of each run, Pallas kernels for 22% -> 23%
where the time goes in v4:
time: 23 us; the launch traced here: 22.8 us
  Pallas kernels  10.1 us (44%)
  starting transfers between devices  9.47 us (41%)
  between operations  2.05 us (9%)
  waiting for transfers between devices  1.01 us (4%)
    ppermute x5, starting transfers between devices, send(): lax.ppermute(array, 'context', [(rank, rank ^ hop) for rank in range(coun...  8.65 us
    pallas_call x2, Pallas kernels, middle(): pl.pallas_call(functools.partial(middle_kernel, (counts, block, WIDE - wi...  3.65 us
    pallas_call x1, Pallas kernels, on_device(): pl.pallas_call(functools.partial(last_kernel, (counts, block, heads, dec,...  3.39 us
    pallas_call x1, Pallas kernels, on_device(): pl.pallas_call(functools.partial(table_kernel, (layout, tok, cached, bloc...  1.67 us
    pallas_call x1, Pallas kernels, on_device(): pl.pallas_call(pack_kernel, out_shape=pltpu.VMEM((rows, LANES), jnp.bfloa...  1.4 us
    ppermute x3, starting transfers between devices, swap(): return lax.ppermute(array, 'tensor', [(0, 1), (1, 0)])  0.82 us
    ppermute x3, waiting for transfers between devices, swap(): return lax.ppermute(array, 'tensor', [(0, 1), (1, 0)])  0.81 us
  transfers between devices with their start and end apart: 8, of which 2 were waited for; matrix products, arithmetic and copies ran while one was open for 1% of the time, Pallas kernels for 23%

profile of v4, /device:TPU:0, one launch (start us, length us, event | category | flops | bytes accessed | tf_op | source)
XLA Modules:
  0.0 22.8 jit_solution(13770233555098774610)
XLA Ops:
  0.6 1.4 %shard_map.122.refs_0_ = bf16[208,128]{1,0:T(8,128)(2,1)S(1)} custom-call(bf16[448,576]{1,0:T(8,128)(2,1)} %down_ref.1, bf16[2,7168]{1,0:T(2,128)(2,1)} %bitcast.9, bf16[1,64,576]{2,1,0:T(8,128)(2,1)} %latent_ref.1, bf16[1,16,576]{2,1,0:T(8,128)(2,1)} %bitcast.10), custom_call_target="tpu_custom_call" | custom-call | tf_op jit(solution)/shard_map/pallas_call | solution.py:367
  2.0 5.1 %collective-permute-start.3 = (bf16[208,128]{1,0:T(8,128)(2,1)S(1)}, bf16[208,128]{1,0:T(8,128)(2,1)S(1)}, u32[]{:S(2)}, u32[]{:S(2)}) collective-permute-start(bf16[208,128]{1,0:T(8,128)(2,1)S(1)} %shard_map.122.refs_0_), channel_id=1, source_target_pairs={{0,12},{2,14},{4,8},{6,10},{8,4},{10,6},{12,0},{14,2},{1,13},{3,15... | collective-permute-start | bytes 159752 | tf_op jit(solution)/shard_map/ppermute | solution.py:376
  7.1 0.0 collective-permute-start.2
  7.1 0.6 %collective-permute-start.1 = (bf16[208,128]{1,0:T(8,128)(2,1)S(1)}, bf16[208,128]{1,0:T(8,128)(2,1)S(1)}, u32[]{:S(2)}, u32[]{:S(2)}) collective-permute-start(bf16[208,128]{1,0:T(8,128)(2,1)S(1)} %shard_map.122.refs_0_), channel_id=1, source_target_pairs={{0,4},{2,6},{4,0},{6,2},{8,12},{10,14},{12,8},{14,10},{1,5},{3,7},... | collective-permute-start | bytes 159752 | tf_op jit(solution)/shard_map/ppermute | solution.py:376
  7.7 1.7 %collective-permute-start = (bf16[208,128]{1,0:T(8,128)(2,1)S(1)}, bf16[208,128]{1,0:T(8,128)(2,1)S(1)}, u32[]{:S(2)}, u32[]{:S(2)}) collective-permute-start(bf16[208,128]{1,0:T(8,128)(2,1)S(1)} %shard_map.122.refs_0_), channel_id=1, source_target_pairs={{0,2},{2,0},{4,6},{6,4},{8,10},{10,8},{12,14},{14,12},{1,3},{3,1},... | collective-permute-start | bytes 159752 | tf_op jit(solution)/shard_map/ppermute | solution.py:376
  10.7 1.7 %shard_map.121 = (bf16[400,128]{1,0:T(8,128)(2,1)S(1)}, bf16[240,128]{1,0:T(8,128)(2,1)S(1)}, f32[2,2,64]{2,1,0:T(2,128)S(1)}, bf16[64,32,64]{2,1,0:T(8,128)(2,1...) custom-call(s32[1]{0:T(128)S(6)} %copy.13.prefix_ref, s32[1]{0:T(128)S(6)} %copy.14.length_ref, ...), custom_call_target="tpu_custom_call" | custom-call | tf_op jit(solution)/shard_map/pallas_call | solution.py:403
  12.4 0.0 slice-start
  12.4 0.0 collective-permute-done.3.refs_2_
  12.4 0.0 collective-permute-done.2.refs_1_
  12.4 0.0 collective-permute-done.1.refs_0_
  12.4 0.0 collective-permute-done.refs_1_
  12.4 1.3 %collective-permute-start.6 = (bf16[3,208,128]{2,1,0:T(8,128)(2,1)S(1)}, bf16[3,208,128]{2,1,0:T(8,128)(2,1)S(1)}, u32[]{:S(2)}, u32[]{:S(2)}) collective-permute-start(bf16[3,208,128]{2,1,0:T(8,128)(2,1)S(1)} %shard_map.123.refs_1_), channel_id=1, source_target_pairs={{0,2},{2,0},{4,6},{6,4},{8,10},{10,8},{12,14},{14,12},{1,3},{3,1},... | collective-permute-start | bytes 479240 | tf_op jit(solution)/shard_map/ppermute | solution.py:376
  13.7 0.0 collective-permute-start.5
  13.7 0.6 %collective-permute-start.4 = (bf16[2,208,128]{2,1,0:T(8,128)(2,1)S(1)}, bf16[2,208,128]{2,1,0:T(8,128)(2,1)S(1)}, u32[]{:S(2)}, u32[]{:S(2)}) collective-permute-start(bf16[2,208,128]{2,1,0:T(8,128)(2,1)S(1)} %shard_map.124.refs_0_), channel_id=1, source_target_pairs={{0,1},{1,0},{2,3},{3,2},{4,5},{5,4},{6,7},{7,6},{8,9},{9,8},{10,11... | collective-permute-start | bytes 319496 | tf_op jit(solution)/shard_map/ppermute | solution.py:379
  14.3 0.0 slice-done
  14.3 0.1 pad_maximum_fusion.late_ref
  14.5 0.0 copy-start
  14.5 0.8 %collective-permute-done.4.refs_2_.refs_3_ = bf16[2,208,128]{2,1,0:T(8,128)(2,1)S(1)} collective-permute-done((bf16[2,208,128]{2,1,0:T(8,128)(2,1)S(1)}, bf16[2,208,128]{2,1,0:T(8,128)(2,1)S(1)}, u32[]{:S(2)}, u32[]{:S(2)}) %collective-permute-start.4) | collective-permute-done | bytes 106528 | tf_op jit(solution)/shard_map/ppermute | solution.py:379
  15.3 0.0 collective-permute-done.5.refs_3_.refs_4_
  15.3 2.3 %shard_map.125 = (f32[3,512,512]{2,1,0:T(8,128)S(1)}, f32[3,8,512]{2,1,0:T(8,128)S(1)}, bf16[400,640]{1,0:T(8,128)(2,1)S(1)}, bf16[512,400]{1,0:T(8,128)(2,1)S(1)}) custom-call(bf16[3,512,640]{2,1,0:T(8,128)(2,1)S(1)} %get-tuple-element.36.marked_ref, bf16[1,512,640]{2,1,0:T(8,128)(2,1)S(1)} %pad_maximum_fusion.late_ref, ...), custom_call_target="tpu_custom_call" | custom-call | tf_op jit(solution)/shard_map/pallas_call | solution.py:453
  17.6 0.0 copy-done
  17.6 0.2 collective-permute-done.6.refs_2_
  17.8 0.2 %collective-permute-start.7 = (bf16[3,208,128]{2,1,0:T(8,128)(2,1)S(1)}, bf16[3,208,128]{2,1,0:T(8,128)(2,1)S(1)}, u32[]{:S(2)}, u32[]{:S(2)}) collective-permute-start(bf16[3,208,128]{2,1,0:T(8,128)(2,1)S(1)} %collective-permute-done.6.refs_2_), channel_id=1, source_target_pairs={{0,1},{1,0},{2,3},{3,2},{4,5},{5,4},{6,7},{7,6},{8,9},{9,8},{10,11... | collective-permute-start | bytes 479240 | tf_op jit(solution)/shard_map/ppermute | solution.py:379
  18.0 1.4 %shard_map.126 = (f32[2,512,512]{2,1,0:T(8,128)S(1)}, f32[2,8,512]{2,1,0:T(8,128)S(1)}) custom-call(bf16[3,512,640]{2,1,0:T(8,128)(2,1)S(1)} %get-tuple-element.36.marked_ref, bf16[1,512,640]{2,1,0:T(8,128)(2,1)S(1)} %pad_maximum_fusion.late_ref, bf16[128,640]{1,0:T(8,128)(2,1)S(1)} %pad.4.decode_ref, bf16[400,128]{1,0:T(8,128)(2,1)S(1)} %get-tuple-element.42.table_ref, ...), custom_call_target="tpu_custom_call" | custom-call | tf_op jit(solution)/shard_map/pallas_call | solution.py:453
  19.4 0.0 collective-permute-done.7.refs_5_
  19.4 3.4 %shard_map.127 = (bf16[1,64,32,512]{3,2,1,0:T(8,128)(2,1)}, bf16[1,2,32,512]{3,2,1,0:T(8,128)(2,1)}, bf16[1,2,576]{2,1,0:T(2,128)(2,1)}) custom-call(bf16[3,512,640]{2,1,0:T(8,128)(2,1)S(1)} %get-tuple-element.36.marked_ref, bf16[1,512,640]{2,1,0:T(8,128)(2,1)S(1)} %pad_maximum_fusion.late_ref, bf16[128,640]{1,0:T(8,128)(2,1)S(1)} %pad.4.decode_ref, ...), custom_call_target="tpu_custom_call" | custom-call | tf_op jit(solution)/shard_map/pallas_call | solution.py:488
  (4 shorter events, 0.0 us)
Async XLA Ops:
  2.0 10.4 %collective-permute-start.3 = (bf16[208,128]{1,0:T(8,128)(2,1)S(1)}, bf16[208,128]{1,0:T(8,128)(2,1)S(1)}, u32[]{:S(2)}, u32[]{:S(2)}) collective-permute-start(bf16[208,128]{1,0:T(8,128)(2,1)S(1)} %shard_map.122.refs_0_), channel_id=1, source_target_pairs={{0,12},{2,14},{4,8},{6,10},{8,4},{10,6},{12,0},{14,2},{1,13},{3,15... | collective-permute-start | bytes 159752 | tf_op jit(solution)/shard_map/ppermute | solution.py:376
  7.1 5.3 %collective-permute-start.2 = (bf16[208,128]{1,0:T(8,128)(2,1)S(1)}, bf16[208,128]{1,0:T(8,128)(2,1)S(1)}, u32[]{:S(2)}, u32[]{:S(2)}) collective-permute-start(bf16[208,128]{1,0:T(8,128)(2,1)S(1)} %shard_map.122.refs_0_), channel_id=1, source_target_pairs={{0,8},{2,10},{4,12},{6,14},{8,0},{10,2},{12,4},{14,6},{1,9},{3,11}... | collective-permute-start | bytes 159752 | tf_op jit(solution)/shard_map/ppermute | solution.py:376
  7.1 5.3 %collective-permute-start.1 = (bf16[208,128]{1,0:T(8,128)(2,1)S(1)}, bf16[208,128]{1,0:T(8,128)(2,1)S(1)}, u32[]{:S(2)}, u32[]{:S(2)}) collective-permute-start(bf16[208,128]{1,0:T(8,128)(2,1)S(1)} %shard_map.122.refs_0_), channel_id=1, source_target_pairs={{0,4},{2,6},{4,0},{6,2},{8,12},{10,14},{12,8},{14,10},{1,5},{3,7},... | collective-permute-start | bytes 159752 | tf_op jit(solution)/shard_map/ppermute | solution.py:376
  7.7 4.7 %collective-permute-start = (bf16[208,128]{1,0:T(8,128)(2,1)S(1)}, bf16[208,128]{1,0:T(8,128)(2,1)S(1)}, u32[]{:S(2)}, u32[]{:S(2)}) collective-permute-start(bf16[208,128]{1,0:T(8,128)(2,1)S(1)} %shard_map.122.refs_0_), channel_id=1, source_target_pairs={{0,2},{2,0},{4,6},{6,4},{8,10},{10,8},{12,14},{14,12},{1,3},{3,1},... | collective-permute-start | bytes 159752 | tf_op jit(solution)/shard_map/ppermute | solution.py:376
  12.4 2.0 %slice-start = ((bf16[1,64,32,576]{3,2,1,0:T(8,128)(2,1)}), bf16[1,16,32,576]{3,2,1,0:T(8,128)(2,1)S(1)}, s32[]{:S(2)}) async-start(bf16[1,64,32,576]{3,2,1,0:T(8,128)(2,1)} %query_hbm.1), calls=%async_computation | async-start | bytes 1310720 | tf_op jit(solution)/shard_map/slice | solution.py:431
  12.4 5.3 %collective-permute-start.6 = (bf16[3,208,128]{2,1,0:T(8,128)(2,1)S(1)}, bf16[3,208,128]{2,1,0:T(8,128)(2,1)S(1)}, u32[]{:S(2)}, u32[]{:S(2)}) collective-permute-start(bf16[3,208,128]{2,1,0:T(8,128)(2,1)S(1)} %shard_map.123.refs_1_), channel_id=1, source_target_pairs={{0,2},{2,0},{4,6},{6,4},{8,10},{10,8},{12,14},{14,12},{1,3},{3,1},... | collective-permute-start | bytes 479240 | tf_op jit(solution)/shard_map/ppermute | solution.py:376
  13.7 1.5 %collective-permute-start.5 = (bf16[3,208,128]{2,1,0:T(8,128)(2,1)S(1)}, bf16[3,208,128]{2,1,0:T(8,128)(2,1)S(1)}, u32[]{:S(2)}, u32[]{:S(2)}) collective-permute-start(bf16[3,208,128]{2,1,0:T(8,128)(2,1)S(1)} %shard_map.123.refs_1_), channel_id=1, source_target_pairs={{0,1},{1,0},{2,3},{3,2},{4,5},{5,4},{6,7},{7,6},{8,9},{9,8},{10,11... | collective-permute-start | bytes 479240 | tf_op jit(solution)/shard_map/ppermute | solution.py:379
  13.7 1.5 %collective-permute-start.4 = (bf16[2,208,128]{2,1,0:T(8,128)(2,1)S(1)}, bf16[2,208,128]{2,1,0:T(8,128)(2,1)S(1)}, u32[]{:S(2)}, u32[]{:S(2)}) collective-permute-start(bf16[2,208,128]{2,1,0:T(8,128)(2,1)S(1)} %shard_map.124.refs_0_), channel_id=1, source_target_pairs={{0,1},{1,0},{2,3},{3,2},{4,5},{5,4},{6,7},{7,6},{8,9},{9,8},{10,11... | collective-permute-start | bytes 319496 | tf_op jit(solution)/shard_map/ppermute | solution.py:379
  14.5 3.1 %copy-start = (bf16[1,2,32,576]{3,2,1,0:T(8,128)(2,1)S(1)}, bf16[1,2,32,576]{3,2,1,0:T(8,128)(2,1)}, u32[]{:S(2)}) copy-start(bf16[1,2,32,576]{3,2,1,0:T(8,128)(2,1)} %param.19) | copy-start | bytes 221188
  17.8 1.6 %collective-permute-start.7 = (bf16[3,208,128]{2,1,0:T(8,128)(2,1)S(1)}, bf16[3,208,128]{2,1,0:T(8,128)(2,1)S(1)}, u32[]{:S(2)}, u32[]{:S(2)}) collective-permute-start(bf16[3,208,128]{2,1,0:T(8,128)(2,1)S(1)} %collective-permute-done.6.refs_2_), channel_id=1, source_target_pairs={{0,1},{1,0},{2,3},{3,2},{4,5},{5,4},{6,7},{7,6},{8,9},{9,8},{10,11... | collective-permute-start | bytes 479240 | tf_op jit(solution)/shard_map/ppermute | solution.py:379
